TPU v7x, 512 devices: a whole 4x8x8 slice. The times are simulated.
512 devices in a mesh: dp: 32 (over z, y_hi), mp: 16 (over y_lo, x, core).
Axes of the slice: x: 4, y: 8 (y_hi: 4, y_lo: 2; y = y_hi * 2 + y_lo), z: 8, core: 2. Of those that a mesh axis runs over, the one named last changes fastest.
Arguments:
- inputs: bfloat16 [384, 256, 4096], P('dp', None, 'mp'), may hold values from -6 to 6
- cotangents: bfloat16 [384, 256, 4096], P('dp', None, 'mp'), may hold values from -6 to 6
- lengths: int32 [384], P('dp'), may hold values from 32 to 256
- reducing_matrix: bfloat16 [128, 4096], P(None, 'mp'), may hold values from -0.09375 to 0.09375
- expanding_matrix: bfloat16 [4096, 128], P('mp'), may hold values from -0.09375 to 0.09375
- width_sign_seeds: int32 [2, 256], replicated, may hold values from 0 to 1073741823
- rank_sign_seeds: int32 [2, 32], replicated, may hold values from 0 to 1073741823
- validation_projected: bfloat16 [2048, 8192], P('dp', 'mp'), may hold values from -6 to 6
Outputs:
- train_proj: float32 [384, 8192], P('dp', 'mp')
- influence: float32 [384, 8], replicated
All inputs are finite; a program needn't handle non-finite values.
Results may differ from a plain program's by a relative error of at most 0.0003.
Values sent between devices are 32-bit elements; how exact they have to be, the bound alone decides.
A program may use at most 64 MiB of HBM per device.

v0:
```python
import math

import jax
import jax.numpy as jnp
from jax import lax
from jax.sharding import PartitionSpec as P

HIDDEN_SIZE = 4096
LOWRANK_DIM = 128
K1 = 32
K2 = 256
K = 8192
SEQUENCE_LEN = 256
TASKS = 8


epsilon = 1e-06


def sign_table(seed_rows, column_ids):
    mixed = seed_rows[:, None] + column_ids[None, :] * 747796405
    for multiplier, distance in ((1103515245, 16), (1664525, 13), (22695477, 16)):
        mixed = mixed & 2147483647
        mixed = mixed ^ jnp.right_shift(mixed, distance)
        mixed = mixed * multiplier
    mixed = mixed & 2147483647
    parity = jnp.right_shift(mixed, 17) & 1
    return (1 - 2 * parity).astype(jnp.float32)


def task_maxima(scores, first_column, per_task):
    column_ids = first_column + jnp.arange(scores.shape[1], dtype=jnp.int32)
    task_of_column = column_ids // per_task
    in_task = task_of_column[:, None] == jnp.arange(TASKS, dtype=jnp.int32)[None, :]
    masked = jnp.where(in_task[None, :, :], scores[:, :, None], -1e30)
    return jnp.max(masked, axis=1)


def on_device(
    inputs,
    cotangents,
    lengths,
    reducing_matrix,
    expanding_matrix,
    width_sign_seeds,
    rank_sign_seeds,
    validation_projected,
):
    examples = inputs.shape[0]
    tok_count = inputs.shape[1]
    shard_width = inputs.shape[2]
    model_index = lax.axis_index("mp")
    top_score = lax.Precision.HIGHEST
    column_ids = model_index * shard_width + jnp.arange(shard_width, dtype=jnp.int32)
    positions = jnp.arange(tok_count, dtype=jnp.int32)
    token_keep = (positions[None, :] < lengths[:, None]).astype(jnp.bfloat16)[:, :, None]
    input_masked = inputs * token_keep
    result_zeroed_pad = cotangents * token_keep
    right_a = sign_table(width_sign_seeds[0], column_ids).astype(jnp.bfloat16)
    right_b = sign_table(width_sign_seeds[1], column_ids).astype(jnp.bfloat16)
    lowrank_coordinate = jnp.arange(reducing_matrix.shape[0], dtype=jnp.int32)
    left_a = sign_table(rank_sign_seeds[0], lowrank_coordinate)
    left_b = sign_table(rank_sign_seeds[1], lowrank_coordinate)
    output_portion = jnp.einsum(
        "rjt,tf->rjf", result_zeroed_pad, expanding_matrix, preferred_element_type=jnp.float32
    )
    input_portion = jnp.einsum(
        "oka,ia->oki", input_masked, reducing_matrix, preferred_element_type=jnp.float32
    )
    projected_input = jnp.einsum(
        "etd,kd->etk", input_masked, right_a, preferred_element_type=jnp.float32
    )
    projected_output = jnp.einsum(
        "etd,kd->etk", result_zeroed_pad, right_b, preferred_element_type=jnp.float32
    )
    adapter_output, adapter_input = lax.psum((output_portion, input_portion), "mp")
    down_inner = jnp.einsum("vdc,vdb->vcb", adapter_output, projected_input, precision=top_score)
    up_inner = jnp.einsum("vdc,vdb->vcb", adapter_input, projected_output, precision=top_score)
    combined = jnp.einsum("ar,erk->eak", left_a, down_inner, precision=top_score)
    combined = combined + jnp.einsum("ar,erk->eak", left_b, up_inner, precision=top_score)
    sketch_multiplier = 1.0 / math.sqrt(2.0 * LOWRANK_DIM * HIDDEN_SIZE * SEQUENCE_LEN)
    partial_value = (combined * sketch_multiplier).reshape(examples, K1 * K2)
    val_wide = validation_projected.astype(jnp.float32)
    val_local = jnp.sum(val_wide * val_wide, axis=1)
    train_proj = lax.psum_scatter(partial_value, "mp", scatter_dimension=1, tiled=True)
    train_sq, val_sq = lax.psum((jnp.sum(train_proj * train_proj, axis=1), val_local), "mp")
    unit_train = train_proj * lax.rsqrt(train_sq + epsilon)[:, None]
    unit_val = val_wide * lax.rsqrt(val_sq + epsilon)[:, None]
    val_total = validation_projected.shape[0] * lax.axis_size("dp")
    per_task = val_total // TASKS
    cosine_scale = math.sqrt(K)
    partial_scores = jnp.einsum(
        "ek,vk->ev",
        unit_train,
        lax.all_gather(unit_val, "dp", axis=0, tiled=True),
        precision=top_score,
    )
    summed_scores = (
        lax.psum_scatter(partial_scores, "mp", scatter_dimension=1, tiled=True) * cosine_scale
    )
    first_column = model_index * summed_scores.shape[1]
    local_best = task_maxima(summed_scores, first_column, per_task)
    merged_best = lax.pmax(local_best, "mp")
    influence = lax.all_gather(merged_best, "dp", axis=0, tiled=True)
    return (train_proj, influence)


def solution(mesh):
    in_specs = (
        P("dp", None, "mp"),
        P("dp", None, "mp"),
        P("dp"),
        P(None, "mp"),
        P("mp", None),
        P(),
        P(),
        P("dp", "mp"),
    )
    out_specs = (P("dp", "mp"), P())
    return jax.shard_map(
        on_device, mesh=mesh, in_specs=in_specs, out_specs=out_specs, check_vma=False
    )
```

profile of v0, /device:TPU:8, one launch (start us, length us, event | category | flops | bytes accessed | tf_op | source)
XLA Modules:
  0.0 550.0 jit_solution(8356261156552752744)
XLA Ops:
  7.2 0.0 all-reduce.4.cloned.1.call-start
  7.2 0.7 fusion.101
  8.0 0.1 copy-done
  8.0 3.4 fusion
  11.4 1.8 fusion.6
  13.2 0.0 reduce-scatter.3.cloned.1.call-start
  13.3 0.6 copy-done.8
  13.9 0.7 copy-done.1
  14.6 2.4 fusion.2
  17.1 0.8 fusion.4
  17.9 135.9 %all-reduce.4.cloned.1.call-done = (f32[12,256,128]{2,1,0:T(8,128)}, f32[12,256,128]{2,1,0:T(8,128)}) async-done(((f32[12,256,128]{2,1,0:T(8,128)}, f32[12,256,128]{2,1,0:T(8,128)}), (f32[12,256,128]{2,1,0:T(8,128)}, f32[12,256,128]{2,1,0:T(8,128)})) %all-reduce.4.cloned.1.call-update) | async-done | bytes 3145744 | tf_op jit(solution)/shard_map/psum | solution.py:76
  153.8 5.2 fusion.161
  159.0 2.9 fusion.162
  161.9 1.0 fusion.81
  162.9 1.0 fusion.9
  164.0 1.1 copy.20
  165.1 0.0 all-gather.3.cloned.1.call-start
  165.2 0.1 fusion.42
  165.3 66.6 %reduce-scatter.3.cloned.1.call-done = f32[12,512]{1,0:T(8,128)} async-done(((f32[12,8192]{1,0:T(8,128)}), f32[12,512]{1,0:T(8,128)}) %reduce-scatter.3.cloned.1.call-update) | async-done | bytes 24592 | tf_op jit(solution)/shard_map/reduce_scatter | solution.py:85
  231.8 0.9 multiply_reduce_fusion
  232.7 28.5 %all-reduce = (f32[64]{0:T(128)S(1)}, f32[12]{0:T(128)S(1)}) all-reduce(f32[64]{0:T(128)S(1)} %fusion.42, f32[12]{0:T(128)S(1)} %multiply_reduce_fusion), channel_id=1, replica_groups=mesh['dp'=32,'mp'=16] {'mp'}, use_global_device_ids=true, to_apply=%region_6.0 | all-reduce | flops 76 | bytes 608 | tf_op jit(solution)/shard_map/psum | solution.py:86
  261.2 0.7 convert_multiply_fusion
  261.9 0.2 reduce-scatter.5.cloned.1.call-start
  262.2 100.6 %all-gather.3.cloned.1.call-done = f32[2048,512]{1,0:T(8,128)} async-done(((f32[64,512]{1,0:T(8,128)}), f32[2048,512]{1,0:T(8,128)}) %all-gather.3.cloned.1.call-update) | async-done | bytes 4194320 | tf_op jit(solution)/shard_map/all_gather | solution.py:95
  362.8 6.4 %fusion.67 = f32[12,2048]{1,0:T(8,128)} fusion(f32[2048,512]{1,0:T(8,128)} %all-gather.3.cloned.1.call-done, f32[12,512]{1,0:T(8,128)} %reduce-scatter.3.cloned.1.call-done, f32[12]{0:T(128)S(1)} %add_rsqrt_fusion.1), kind=kOutput, calls=%fused_computation.75 | convolution fusion | flops 151001088 | bytes 4317232 | tf_op jit(solution)/shard_map/ek,vk->ev/dot_general | solution.py:92
  369.2 61.4 %reduce-scatter.5.cloned.1.call-done = f32[12,128]{1,0:T(8,128)} async-done(((f32[12,2048]{1,0:T(8,128)}), f32[12,128]{1,0:T(8,128)}) %reduce-scatter.5.cloned.1.call-update) | async-done | bytes 6160 | tf_op jit(solution)/shard_map/reduce_scatter | solution.py:99
  430.6 0.7 broadcast_multiply_fusion
  431.3 0.1 select_reduce_fusion
  431.4 29.0 %pmax.7 = f32[12,8]{1,0:T(8,128)S(1)} all-reduce(f32[12,8]{1,0:T(8,128)S(1)} %select_reduce_fusion), channel_id=1, replica_groups=mesh['dp'=32,'mp'=16] {'mp'}, use_global_device_ids=true, to_apply=%region_9.10 | all-reduce | flops 96 | bytes 768 | tf_op jit(solution)/shard_map/pmax | solution.py:103
  460.4 0.1 copy.16
  460.5 82.2 %all-gather = f32[32,12,8]{1,2,0:T(8,128)S(1)} all-gather(f32[1,12,8]{1,2,0:T(8,128)S(1)} %bitcast.41), channel_id=1, replica_groups=mesh['dp'=32,'mp'=16] {'dp'}, dimensions={0}, use_global_device_ids=true | all-gather | bytes 12672 | tf_op jit(solution)/shard_map/all_gather | solution.py:104
  542.8 0.7 reshape.87
  (29 shorter events, 0.2 us)
Async XLA Ops:
  7.2 0.8 copy-start
  7.2 146.6 %all-reduce.4.cloned.1.call-start = ((), (), s32[]{:S(2)}) async-start(), calls=%async_computation.5 | async-start | bytes 6291456 | tf_op jit(solution)/shard_map/psum | solution.py:76
  8.0 3.4 copy-start.2
  8.0 3.4 copy-start.6
  13.2 0.7 copy-start.8
  13.2 0.7 copy-start.7
  13.2 1.4 copy-start.1
  13.2 218.6 %reduce-scatter.3.cloned.1.call-start = ((), (), s32[]{:S(2)}) async-start(), calls=%async_computation.2 | async-start | bytes 557056 | tf_op jit(solution)/shard_map/reduce_scatter | solution.py:85
  14.6 2.5 copy-start.3
  153.8 5.2 copy-start.4
  163.9 1.2 copy-start.5
  165.1 197.7 %all-gather.3.cloned.1.call-start = ((), (), s32[]{:S(2)}) async-start(), calls=%async_computation.3 | async-start | bytes 4325376 | tf_op jit(solution)/shard_map/all_gather | solution.py:95
  261.9 168.7 %reduce-scatter.5.cloned.1.call-start = ((), (), s32[]{:S(2)}) async-start(), calls=%async_computation.4 | async-start | bytes 139264 | tf_op jit(solution)/shard_map/reduce_scatter | solution.py:99
Sparse Core Ops, SparseCore 0:
  13.3 140.4 all-reduce.3
  165.2 66.5 reduce-scatter.2
  262.1 100.7 all-gather.2
  369.3 61.2 reduce-scatter.4
where the time goes:
time: 550 us
  waiting for transfers between devices  365 us (66%)
  blocking collectives  140 us (25%)
  matrix products  24.8 us (5%)
  between operations  13.9 us (3%)
    psum x1, waiting for transfers between devices, on_device(): lax.psum((output_portion, input_portion), 'mp')  136 us
    all_gather x1, waiting for transfers between devices, on_device(): lax.all_gather(unit_val, 'dp', axis=0, tiled=True)  101 us
    all_gather x1, blocking collectives, on_device(): influence = lax.all_gather(merged_best, 'dp', axis=0, tiled=True)  82.2 us
    reduce_scatter x1, waiting for transfers between devices, on_device(): lax.psum_scatter(partial_value, 'mp', scatter_dimension=1, tiled=True)  66.6 us
    reduce_scatter x1, waiting for transfers between devices, on_device(): lax.psum_scatter(partial_scores, 'mp', scatter_dimension=1, tiled=True)  61.4 us
    pmax x1, blocking collectives, on_device(): merged_best = lax.pmax(local_best, 'mp')  29 us
    psum x1, blocking collectives, on_device(): lax.psum((jnp.sum(train_proj * train_proj, axis=1), val_local), 'mp')  28.5 us
  transfers between devices with their start and end apart: 4, of which 4 were waited for; matrix products, arithmetic and copies ran while one was open for 1% of the time, Pallas kernels for 0%

commit v1 on v0

v1 whole, which is shorter than its diff:
```python
import functools
import math

import jax
import jax.numpy as jnp
from jax import lax
from jax.experimental import pallas as pl
from jax.experimental.pallas import tpu as pltpu
from jax.sharding import PartitionSpec as P

MESH = pl.DeviceIdType.MESH
EPSILON = 1e-06
LOWEST = -3e38
F32 = jnp.float32
BF16 = jnp.bfloat16

NT = (((1,), (1,)), ((), ()))
NN = (((1,), (0,)), ((), ()))


def sign_of(seeds, columns):
    mixed = seeds + columns * 747796405
    for multiplier, distance in ((1103515245, 16), (1664525, 13), (22695477, 16)):
        mixed = mixed & 2147483647
        mixed = mixed ^ jnp.right_shift(mixed, distance)
        mixed = mixed * multiplier
    mixed = mixed & 2147483647
    parity = jnp.right_shift(mixed, 17) & 1
    return (1 - 2 * parity).astype(F32)


def dot(a, b, dims):
    return lax.dot_general(a, b, dims, preferred_element_type=F32)


def split(value):
    high = value.astype(BF16)
    return high, (value - high.astype(F32)).astype(BF16)


def kernel(
    nz,
    nyh,
    nq,
    scale,
    root_k,
    x_ref,
    g_ref,
    len_ref,
    red_ref,
    exp_ref,
    wseed_ref,
    rseed_ref,
    val_ref,
    tp_ref,
    inf_ref,
    x_v,
    g_v,
    red_v,
    exp_v,
    wseed_v,
    rseed_v,
    rpad,
    val_v,
    u,
    r1,
    r2,
    uf,
    ra,
    rb,
    ha,
    hb,
    t,
    ts,
    r3,
    r4,
    tg,
    lt,
    vf,
    vb,
    sc,
    r5,
    fy,
    fz,
    in_sem,
    small_sem,
    s1,
    d1,
    s2,
    d2,
    s3,
    d3,
    s4,
    d4,
    s5,
    d5,
    s6,
    d6,
    s7,
    d7,
    sv,
    dv,
    s8,
    d8,
    s9,
    d9,
    s10,
    d10,
    s11,
    d11,
):
    nmp = 2 * nq
    el = x_v.shape[0]
    k1 = nmp * 2
    per = 2 * k1
    half_e = el // 2
    half_rows = half_e * per
    chunk = half_rows // nq
    tokens = x_v.shape[1]
    width = x_v.shape[2]
    vl = val_v.shape[0]
    te = 2 * el
    er = nyh * el // nmp
    hv = nz * vl // 2

    dp = lax.axis_index("dp")
    m = lax.axis_index("mp")
    q = lax.div(m, 2)
    c = lax.rem(m, 2)
    other = 1 - c
    z = lax.div(dp, nyh)
    yh = lax.rem(dp, nyh)
    sibling = (dp, 2 * q + other)

    def chip(p):
        return (dp, 2 * p + c)

    def plane(zz):
        return (zz * nyh + yh, m)

    def row(yy):
        return (z * nyh + yy, m)

    def remote(src, dst, send, recv, device):
        return pltpu.make_async_remote_copy(
            src_ref=src, dst_ref=dst, send_sem=send, recv_sem=recv, device_id=device, device_id_type=MESH
        )

    def input_copies(e):
        return (
            pltpu.make_async_copy(x_ref.at[e], x_v.at[e], in_sem.at[0, e]),
            pltpu.make_async_copy(g_ref.at[e], g_v.at[e], in_sem.at[1, e]),
        )

    small = [
        pltpu.make_async_copy(a, b, small_sem.at[i])
        for i, (a, b) in enumerate(
            (
                (rseed_ref, rseed_v),
                (red_ref, red_v),
                (exp_ref, exp_v),
                (val_ref, val_v),
                (wseed_ref, wseed_v),
            )
        )
    ]
    for copy in small:
        copy.start()

    def order(i):
        return lax.rem(other * half_e + i, el)

    def start_inputs(i, carry):
        for copy in input_copies(order(i)):
            copy.start()
        return carry

    lax.fori_loop(0, el, start_inputs, 0)

    barrier = pltpu.get_barrier_semaphore()

    def greet(device):
        pl.semaphore_signal(barrier, inc=1, device_id=device, device_id_type=MESH)

    def greet_mp(j, carry):
        greet((dp, lax.rem(m + j, nmp)))
        return carry

    lax.fori_loop(1, nmp, greet_mp, 0)
    for j in range(1, nz):
        greet(plane(lax.rem(z + j, nz)))
    for j in range(1, nyh):
        greet(row(lax.rem(yh + j, nyh)))

    small[0].wait()
    rpad[...] = jnp.zeros_like(rpad)
    rpad[0:2, 0:k1] = rseed_v[...]
    ranks = lax.broadcasted_iota(jnp.int32, (128, 128), 0)
    left_a = sign_of(rpad[0:1, :], ranks).T[0:k1].astype(BF16)
    left_b = sign_of(rpad[1:2, :], ranks).T[0:k1].astype(BF16)
    small[1].wait()
    small[2].wait()
    p_out = jnp.concatenate(split(dot(left_a, exp_v[...], NT)), axis=0)
    p_in = jnp.concatenate(split(dot(left_b, red_v[...], NN)), axis=0)

    lane_t = lax.broadcasted_iota(jnp.int32, (k1, tokens), 1)

    def sketch(i, carry):
        e = order(i)
        for copy in input_copies(e):
            copy.wait()
        kept = lane_t < len_ref[e]
        out = dot(p_out, g_v[e], NT)
        inn = dot(p_in, x_v[e], NT)
        base = pl.multiple_of(e * per, per)
        u[pl.ds(base, k1), :] = jnp.where(kept, out[:k1] + out[k1:], 0.0)
        u[pl.ds(base + k1, k1), :] = jnp.where(kept, inn[:k1] + inn[k1:], 0.0)
        return carry

    def u_half(h):
        return u.at[pl.ds(pl.multiple_of(h * half_rows, half_rows), half_rows)]

    def rows_of(h, p):
        return pl.ds(pl.multiple_of(h * half_rows + p * chunk, chunk), chunk)

    lax.fori_loop(0, half_e, sketch, 0)

    pl.semaphore_wait(barrier, (nmp - 1) + (nz - 1) + (nyh - 1))

    to_sibling = remote(u_half(other), r1, s1.at[0], d1.at[0], sibling)
    to_sibling.start()

    small[3].wait()
    vf[z] = val_v[...].astype(F32)
    steps = nz // 2
    up = plane(lax.rem(z + 1, nz))
    down = plane(lax.rem(z + nz - 1, nz))

    def ring(step):
        a = lax.rem(z + nz - step, nz)
        b = lax.rem(z + step, nz)
        if step < steps - 1:
            first, second = vf.at[a], vf.at[b]
        else:
            first, second = vf.at[a, pl.ds(0, vl // 2)], vf.at[b, pl.ds(vl // 2, vl // 2)]
        return (
            remote(first, first, sv.at[0, step], dv.at[0, step], up),
            remote(second, second, sv.at[1, step], dv.at[1, step], down),
        )

    def ring_start(step):
        for copy in ring(step):
            copy.start()

    def ring_wait(step):
        for copy in ring(step):
            copy.wait_recv()

    ring_start(0)

    lax.fori_loop(half_e, el, sketch, 0)

    to_sibling.wait_recv()

    def spread(j):
        p = lax.rem(q + j, nq)
        return remote(u.at[rows_of(c, p)], r2.at[j - 1], s2.at[j - 1], d2.at[j - 1], chip(p))

    for j in range(1, nq):
        p = lax.rem(q + j, nq)
        u[rows_of(c, p), :] += r1[pl.ds(pl.multiple_of(p * chunk, chunk), chunk), :]
        spread(j).start()
    ring_wait(0)
    if steps > 1:
        ring_start(1)

    small[4].wait()
    columns = m * width + lax.broadcasted_iota(jnp.int32, (width, wseed_v.shape[1]), 0)
    ra[...] = sign_of(wseed_v[0:1, :], columns).astype(BF16)
    rb[...] = sign_of(wseed_v[1:2, :], columns).astype(BF16)

    own = u[rows_of(c, q), :] + r1[pl.ds(pl.multiple_of(q * chunk, chunk), chunk), :]
    for j in range(1, nq):
        spread(j).wait_recv()
        own = own + r2[j - 1]
    uf[rows_of(c, q), :] = own

    def hand_out(j):
        part = uf.at[rows_of(c, q)]
        return remote(part, part, s3.at[j - 1], d3.at[j - 1], chip(lax.rem(q + j, nq)))

    def landed(j):
        part = uf.at[rows_of(c, lax.rem(q + nq - j, nq))]
        return remote(part, part, s3.at[j - 1], d3.at[j - 1], chip(lax.rem(q + nq - j, nq)))

    def pass_on(j):
        part = uf.at[rows_of(c, lax.rem(q + nq - j, nq))]
        return remote(part, part, s4.at[j], d4.at[j], sibling)

    def passed(j):
        part = uf.at[rows_of(other, lax.rem(q + nq - j, nq))]
        return remote(part, part, s4.at[j], d4.at[j], sibling)

    for j in range(1, nq):
        hand_out(j).start()
    pass_on(0).start()
    if steps > 1:
        ring_wait(1)
    if steps > 2:
        ring_start(2)
    for j in range(1, nq):
        landed(j).wait_recv()
        pass_on(j).start()

    def project(first):
        def body(i, carry):
            e = first + i
            base = pl.multiple_of(e * per, per)
            a = jnp.concatenate(split(uf[pl.ds(base, k1), :]), axis=0)
            b = jnp.concatenate(split(uf[pl.ds(base + k1, k1), :]), axis=0)
            down_part = dot(a, x_v[e], NN)
            up_part = dot(b, g_v[e], NN)
            at = pl.ds(pl.multiple_of(e * k1, k1), k1)
            high, low = split(down_part[:k1] + down_part[k1:])
            ha[0, at, :] = high
            ha[1, at, :] = low
            high, low = split(up_part[:k1] + up_part[k1:])
            hb[0, at, :] = high
            hb[1, at, :] = low
            return carry

        return body

    lax.fori_loop(0, half_e, project(c * half_e), 0)
    for j in range(nq):
        passed(j).wait_recv()
    if steps > 2:
        ring_wait(2)
    if steps > 3:
        ring_start(3)
    lax.fori_loop(0, half_e, project(other * half_e), 0)

    block = el * k1 // 3

    def combine(i, carry):
        at = pl.ds(pl.multiple_of(i * block, block), block)
        total = dot(ha[0, at, :], ra[...], NN) + dot(hb[0, at, :], rb[...], NN)
        total = total + (dot(ha[1, at, :], ra[...], NN) + dot(hb[1, at, :], rb[...], NN))
        total = total * scale
        t[0, at, :] = total[:, :128]
        t[1, at, :] = total[:, 128:]
        return carry

    lax.fori_loop(0, 3, combine, 0)
    for a in range(k1):
        cc, qq, al = (a // 2) % 2, a // 4, a % 2
        for side in range(2):
            ts[cc, qq, al * el : (al + 1) * el, side * 128 : (side + 1) * 128] = t[
                side, pl.ds(a, el, stride=k1), :
            ]

    swap = remote(ts.at[other], r3, s5.at[0], d5.at[0], sibling)
    swap.start()
    if steps > 3:
        ring_wait(3)

    swap.wait_recv()

    def scatter(j):
        p = lax.rem(q + j, nq)
        return remote(ts.at[c, p], r4.at[j - 1], s6.at[j - 1], d6.at[j - 1], chip(p))

    for j in range(1, nq):
        p = lax.rem(q + j, nq)
        ts[c, p] += r3[p]
        scatter(j).start()

    def narrow(i, carry):
        vb[pl.ds(pl.multiple_of(i * vl, vl), vl), :] = vf[i].astype(BF16)
        return carry

    lax.fori_loop(0, nz, narrow, 0)
    ones = jnp.ones((16, vf.shape[2]), BF16)
    sc[...] = jnp.zeros_like(sc)
    for side in range(2):
        wide = vb[side * hv : (side + 1) * hv, :].astype(F32)
        high, low = split(wide * wide)
        norms = dot(ones, high, NT) + dot(ones, low, NT)

        def place(i, carry, norms=norms, side=side):
            sc[i, 2 * er + side : 2 * er + side + 1, 0:hv] = norms[0:1]
            return carry

        lax.fori_loop(0, nmp, place, 0)

    total = ts[c, q] + r3[q]
    for j in range(1, nq):
        scatter(j).wait_recv()
        total = total + r4[j - 1]
    tg[yh] = total
    tp_ref[:, 0:256] = total[0:el]
    tp_ref[:, 256:512] = total[el:te]

    def share(j):
        part = tg.at[yh]
        return remote(part, part, s7.at[j - 1], d7.at[j - 1], row(lax.rem(yh + j, nyh)))

    def shared(j):
        part = tg.at[lax.rem(yh + nyh - j, nyh)]
        return remote(part, part, s7.at[j - 1], d7.at[j - 1], row(lax.rem(yh + nyh - j, nyh)))

    for j in range(1, nyh):
        share(j).start()
    for j in range(1, nyh):
        shared(j).wait_recv()

    for y in range(nyh):
        for al in range(2):
            lt[y * el : (y + 1) * el, al * 256 : (al + 1) * 256] = tg[y, al * el : (al + 1) * el, :]
    train = lt[...]
    rows = nyh * el
    high, low = split(train)
    scores = dot(high, vb[...], NT) + dot(low, vb[...], NT)
    squares = jnp.broadcast_to(jnp.sum(train * train, axis=1, keepdims=True), (rows, 128))
    for i in range(nmp):
        sc[i, 0:er, 0:hv] = scores[i * er : (i + 1) * er, 0:hv]
        sc[i, er : 2 * er, 0:hv] = scores[i * er : (i + 1) * er, hv : 2 * hv]
        sc[i, 0:er, hv : hv + 128] = squares[i * er : (i + 1) * er]
        sc[i, er : 2 * er, hv : hv + 128] = squares[i * er : (i + 1) * er]

    def deal(j):
        p = lax.rem(m + j, nmp)
        return remote(sc.at[p], r5.at[j - 1], s8.at[j - 1], d8.at[j - 1], (dp, p))

    def deal_start(j, carry):
        deal(j).start()
        return carry

    def deal_wait(j, carry):
        deal(j).wait_recv()
        return carry + r5[j - 1]

    lax.fori_loop(1, nmp, deal_start, 0)
    summed = lax.fori_loop(1, nmp, deal_wait, sc[m])

    row_id = lax.broadcasted_iota(jnp.int32, (8, hv), 0)
    lane_id = lax.broadcasted_iota(jnp.int32, (8, hv), 1)
    norms = jnp.where(row_id < er, summed[2 * er : 2 * er + 1, 0:hv], summed[2 * er + 1 : 2 * er + 2, 0:hv])
    cosines = summed[:, 0:hv] * lax.rsqrt(norms + EPSILON)
    weight = lax.rsqrt(summed[:, hv : hv + 1] + EPSILON) * root_k
    row_o = lax.broadcasted_iota(jnp.int32, (8, 128), 0)
    lane_o = lax.broadcasted_iota(jnp.int32, (8, 128), 1)
    placed = jnp.full((8, 128), LOWEST, F32)
    first_half = row_o < er
    e_of = jnp.where(first_half, row_o, row_o - er)
    for g in range(nz // 2):
        here = (lane_id >= g * vl) & (lane_id < (g + 1) * vl)
        best = jnp.max(jnp.where(here, cosines, LOWEST), axis=1, keepdims=True) * weight
        lane = e_of * nz + jnp.where(first_half, 0, nz // 2) + g
        placed = jnp.where((lane_o == lane) & (row_o < 2 * er), best, placed)
    fy[0] = jnp.max(placed, axis=0, keepdims=True)

    def merge(j):
        return remote(fy.at[0], fy.at[j], s9.at[j - 1], d9.at[j - 1], row(lax.rem(yh + j, nyh)))

    for j in range(1, nyh):
        merge(j).start()
    best = fy[0]
    for j in range(1, nyh):
        merge(j).wait_recv()
        best = jnp.maximum(best, fy[j])
    fz[z, m] = best

    def tell(j):
        part = fz.at[z, m]
        return remote(part, part, s10.at[j - 1], d10.at[j - 1], (dp, lax.rem(m + j, nmp)))

    def told(j):
        p = lax.rem(m + nmp - j, nmp)
        part = fz.at[z, p]
        return remote(part, part, s10.at[j - 1], d10.at[j - 1], (dp, p))

    def tell_start(j, carry):
        tell(j).start()
        return carry

    def told_wait(j, carry):
        told(j).wait_recv()
        return carry

    lax.fori_loop(1, nmp, tell_start, 0)
    lax.fori_loop(1, nmp, told_wait, 0)

    def publish(j):
        part = fz.at[z]
        return remote(part, part, s11.at[j - 1], d11.at[j - 1], plane(lax.rem(z + j, nz)))

    def published(j):
        zz = lax.rem(z + nz - j, nz)
        part = fz.at[zz]
        return remote(part, part, s11.at[j - 1], d11.at[j - 1], plane(zz))

    for j in range(1, nz):
        publish(j).start()
    for j in range(1, nz):
        published(j).wait_recv()
    inf_ref[...] = fz[...]

    to_sibling.wait_send()
    swap.wait_send()
    for j in range(1, nq):
        spread(j).wait_send()
        hand_out(j).wait_send()
        scatter(j).wait_send()
    for j in range(nq):
        pass_on(j).wait_send()
    for step in range(steps):
        for copy in ring(step):
            copy.wait_send()
    for j in range(1, nyh):
        share(j).wait_send()
        merge(j).wait_send()
    for j in range(1, nz):
        publish(j).wait_send()

    def last(j, carry):
        deal(j).wait_send()
        tell(j).wait_send()
        return carry

    lax.fori_loop(1, nmp, last, 0)


def on_device(nz, nyh, nq, scale, root_k, *args):
    inputs, _, _, reducing, expanding, wseeds, rseeds, validation = args
    el, tokens, width = inputs.shape
    nmp = 2 * nq
    k1 = 2 * nmp
    vl, kl = validation.shape
    k2 = wseeds.shape[1]
    half_rows = el * k1
    chunk = half_rows // nq
    hv = nz * vl // 2
    dma = pltpu.SemaphoreType.DMA
    anywhere = pl.BlockSpec(memory_space=pl.ANY)
    vmem = pl.BlockSpec(memory_space=pltpu.VMEM)
    scratch = [
        pltpu.VMEM(inputs.shape, BF16),
        pltpu.VMEM(inputs.shape, BF16),
        pltpu.VMEM(reducing.shape, BF16),
        pltpu.VMEM(expanding.shape, BF16),
        pltpu.VMEM(wseeds.shape, jnp.int32),
        pltpu.VMEM(rseeds.shape, jnp.int32),
        pltpu.VMEM((8, 128), jnp.int32),
        pltpu.VMEM(validation.shape, BF16),
        pltpu.VMEM((2 * half_rows, tokens), F32),
        pltpu.VMEM((half_rows, tokens), F32),
        pltpu.VMEM((nq - 1, chunk, tokens), F32),
        pltpu.VMEM((2 * half_rows, tokens), F32),
        pltpu.VMEM((width, k2), BF16),
        pltpu.VMEM((width, k2), BF16),
        pltpu.VMEM((2, el * k1, width), BF16),
        pltpu.VMEM((2, el * k1, width), BF16),
        pltpu.VMEM((2, el * k1, 128), F32),
        pltpu.VMEM((2, nq, 2 * el, k2), F32),
        pltpu.VMEM((nq, 2 * el, k2), F32),
        pltpu.VMEM((nq - 1, 2 * el, k2), F32),
        pltpu.VMEM((nyh, 2 * el, k2), F32),
        pltpu.VMEM((nyh * el, kl), F32),
        pltpu.VMEM((nz, vl, kl), F32),
        pltpu.VMEM((nz * vl, kl), BF16),
        pltpu.VMEM((nmp, 8, hv + 128), F32),
        pltpu.VMEM((nmp - 1, 8, hv + 128), F32),
        pltpu.VMEM((nyh, 1, 128), F32),
        pltpu.VMEM((nz, nmp, 1, 128), F32),
        dma((2, el)),
        dma((5,)),
    ]
    ring = (2, nz // 2)
    for count in (
        (1,),
        (nq - 1,),
        (nq - 1,),
        (nq,),
        (1,),
        (nq - 1,),
        (max(nyh - 1, 1),),
        ring,
        (nmp - 1,),
        (max(nyh - 1, 1),),
        (nmp - 1,),
        (nz - 1,),
    ):
        scratch += [dma(count), dma(count)]
    train_proj, best = pl.pallas_call(
        functools.partial(kernel, nz, nyh, nq, scale, root_k),
        out_shape=(
            jax.ShapeDtypeStruct((el, kl), F32),
            jax.ShapeDtypeStruct((nz, nmp, 1, 128), F32),
        ),
        in_specs=[
            anywhere,
            anywhere,
            pl.BlockSpec(memory_space=pltpu.SMEM),
            anywhere,
            anywhere,
            anywhere,
            anywhere,
            anywhere,
        ],
        out_specs=(vmem, vmem),
        scratch_shapes=scratch,
        compiler_params=pltpu.CompilerParams(
            collective_id=0, has_side_effects=True, vmem_limit_bytes=48 * 1024 * 1024
        ),
    )(*args)
    er = nyh * el // nmp
    influence = best.reshape(nz * nmp, 128)[:, : er * nz].reshape(nz * nmp * er, nz)
    return (train_proj, influence)


def solution(mesh, nyh=4):
    ndp, nmp = mesh.shape["dp"], mesh.shape["mp"]
    nz, nq = ndp // nyh, nmp // 2
    width = nmp * 256
    scale = 1.0 / math.sqrt(2.0 * 128 * width * 256)
    root_k = math.sqrt(2 * nmp * 256)
    in_specs = (
        P("dp", None, "mp"),
        P("dp", None, "mp"),
        P("dp"),
        P(None, "mp"),
        P("mp", None),
        P(),
        P(),
        P("dp", "mp"),
    )
    return jax.shard_map(
        functools.partial(on_device, nz, nyh, nq, scale, root_k),
        mesh=mesh,
        in_specs=in_specs,
        out_specs=(P("dp", "mp"), P()),
        check_vma=False,
    )
```

time: 550 us -> 79.9 us (0.15)
  the two profiles are of different devices: /device:TPU:8 before, /device:TPU:1 now
where the time goes in v1:
time: 79.9 us; the launch traced here: 79.6 us
  Pallas kernels  70.2 us (88%)
  local copies, waits for them, and re-layouts  8.76 us (11%)
    pallas_call x1, Pallas kernels, on_device(): pl.pallas_call(functools.partial(kernel, nz, nyh, nq, scale, root_k), out...  70.2 us
    unnamed x18, local copies, waits for them, and re-layouts  8.66 us

profile of v1, /device:TPU:1, one launch (start us, length us, event | category | flops | bytes accessed | tf_op | source)
XLA Modules:
  0.0 79.6 jit_solution(4031001886896769586)
XLA Ops:
  0.6 0.0 copy-start
  0.6 1.4 %copy-done = bf16[12,256,256]{2,1,0:T(8,128)(2,1)S(1)} copy-done((bf16[12,256,256]{2,1,0:T(8,128)(2,1)S(1)}, bf16[12,256,256]{2,1,0:T(8,128)(2,1)}, u32[]{:S(2)}) %copy-start) | copy-done | bytes 1572888
  2.0 0.0 copy-start.1
  2.0 1.4 %copy-done.1 = bf16[12,256,256]{2,1,0:T(8,128)(2,1)S(1)} copy-done((bf16[12,256,256]{2,1,0:T(8,128)(2,1)S(1)}, bf16[12,256,256]{2,1,0:T(8,128)(2,1)}, u32[]{:S(2)}) %copy-start.1) | copy-done | bytes 1572888
  3.5 0.0 copy-start.2
  3.5 0.8 %copy-done.2 = bf16[128,256]{1,0:T(8,128)(2,1)S(1)} copy-done((bf16[128,256]{1,0:T(8,128)(2,1)S(1)}, bf16[128,256]{1,0:T(8,128)(2,1)}, u32[]{:S(2)}) %copy-start.2) | copy-done | bytes 65560
  4.3 0.0 copy-start.3
  4.3 0.8 %copy-done.3 = bf16[256,128]{1,0:T(8,128)(2,1)S(1)} copy-done((bf16[256,128]{1,0:T(8,128)(2,1)S(1)}, bf16[256,128]{1,0:T(8,128)(2,1)}, u32[]{:S(2)}) %copy-start.3) | copy-done | bytes 65560
  5.1 0.0 copy-start.4
  5.1 0.8 %copy-done.4 = bf16[64,512]{1,0:T(8,128)(2,1)S(1)} copy-done((bf16[64,512]{1,0:T(8,128)(2,1)S(1)}, bf16[64,512]{1,0:T(8,128)(2,1)}, u32[]{:S(2)}) %copy-start.4) | copy-done | bytes 65560
  6.0 0.0 copy-start.5
  6.0 0.7 copy-done.5
  6.7 0.0 copy-start.6
  6.7 0.7 copy-done.6
  7.3 0.0 copy-start.7
  7.3 0.7 copy-done.7
  8.0 70.2 %shard_map.95 = (f32[12,512]{1,0:T(8,128)S(1)}, f32[8,16,1,128]{3,2,1,0:T(1,128)S(1)}) custom-call(bf16[12,256,256]{2,1,0:T(8,128)(2,1)S(1)} %copy-done, bf16[12,256,256]{2,1,0:T(8,128)(2,1)S(1)} %copy-done.1, s32[12]{0:T(128)S(1)} %copy-done.7, bf16[128,256]{1,0:T(8,128)(2,1)S(1)} %copy-done.2, bf16[256,128]{1,0:T(8,128)(2,1)S(1)} %copy-done.3, ...), custom_call_target="tpu_custom_call" | custom-call | tf_op jit(solution)/shard_map/pallas_call | solution.py:595
  78.2 0.1 reshape.11
  78.3 0.7 copy.10
  79.0 0.6 copy.12
Async XLA Ops:
  0.6 1.4 %copy-start = (bf16[12,256,256]{2,1,0:T(8,128)(2,1)S(1)}, bf16[12,256,256]{2,1,0:T(8,128)(2,1)}, u32[]{:S(2)}) copy-start(bf16[12,256,256]{2,1,0:T(8,128)(2,1)} %x_ref.1) | copy-start | bytes 4718596
  2.0 1.4 %copy-start.1 = (bf16[12,256,256]{2,1,0:T(8,128)(2,1)S(1)}, bf16[12,256,256]{2,1,0:T(8,128)(2,1)}, u32[]{:S(2)}) copy-start(bf16[12,256,256]{2,1,0:T(8,128)(2,1)} %g_ref.1) | copy-start | bytes 4718596
  3.5 0.8 %copy-start.2 = (bf16[128,256]{1,0:T(8,128)(2,1)S(1)}, bf16[128,256]{1,0:T(8,128)(2,1)}, u32[]{:S(2)}) copy-start(bf16[128,256]{1,0:T(8,128)(2,1)} %red_ref.1) | copy-start | bytes 196612
  4.3 0.8 %copy-start.3 = (bf16[256,128]{1,0:T(8,128)(2,1)S(1)}, bf16[256,128]{1,0:T(8,128)(2,1)}, u32[]{:S(2)}) copy-start(bf16[256,128]{1,0:T(8,128)(2,1)} %exp_ref.1) | copy-start | bytes 196612
  5.1 0.8 %copy-start.4 = (bf16[64,512]{1,0:T(8,128)(2,1)S(1)}, bf16[64,512]{1,0:T(8,128)(2,1)}, u32[]{:S(2)}) copy-start(bf16[64,512]{1,0:T(8,128)(2,1)} %val_ref.1) | copy-start | bytes 196612
  6.0 0.7 copy-start.5
  6.7 0.7 copy-start.6
  7.3 0.7 copy-start.7

commit v2 on v1

v2 whole, which is shorter than its diff:
```python
import functools
import math

import jax
import jax.numpy as jnp
from jax import lax
from jax.experimental import pallas as pl
from jax.experimental.pallas import tpu as pltpu
from jax.sharding import PartitionSpec as P

MESH = pl.DeviceIdType.MESH
EPSILON = 1e-06
LOWEST = -3e38
F32 = jnp.float32
BF16 = jnp.bfloat16

NT = (((1,), (1,)), ((), ()))
NN = (((1,), (0,)), ((), ()))


def sign_of(seeds, columns):
    mixed = seeds + columns * 747796405
    for multiplier, distance in ((1103515245, 16), (1664525, 13), (22695477, 16)):
        mixed = mixed & 2147483647
        mixed = mixed ^ jnp.right_shift(mixed, distance)
        mixed = mixed * multiplier
    mixed = mixed & 2147483647
    parity = jnp.right_shift(mixed, 17) & 1
    return (1 - 2 * parity).astype(F32)


def dot(a, b, dims):
    return lax.dot_general(a, b, dims, preferred_element_type=F32)


def split(value):
    high = value.astype(BF16)
    return high, (value - high.astype(F32)).astype(BF16)


def kernel(nz, nyh, nq, np_, scale, root_k, *refs):
    (
        (x_ref, g_ref, len_ref, red_ref, exp_ref, wseed_ref, rseed_ref, val_ref, tp_ref, inf_ref),
        (x_v, g_v, len_v, red_v, exp_v, wseed_v, rseed_v, rpad, val_v, u, r1, r2, uf, ra, rb, ha, hb, t, ts, r3, r4),
        (tg, lt, vf, vb, vq, rq, sc, r5, fp, fz),
        (in_sem, small_sem, s1, d1, s2, d2, s3, d3, s4, d4, s5, d5, s6, d6, s7, d7, sv, dv, sq, dq, s8, d8, s9, d9, s10, d10),
    ) = refs[:10], refs[10:31], refs[31:41], refs[41:]
    nmp = 2 * nq
    el = x_v.shape[0]
    k1 = nmp * 2
    per = 2 * k1
    half_e = el // 2
    piece_e = half_e // np_
    half_rows = half_e * per
    piece_rows = piece_e * per
    chunk = piece_rows // nq
    tokens = x_v.shape[1]
    width = x_v.shape[2]
    vl = val_v.shape[0]
    te = 2 * el
    er = nyh * el // nmp
    hv = nz * vl // 2

    dp = lax.axis_index("dp")
    m = lax.axis_index("mp")
    q = lax.div(m, 2)
    c = lax.rem(m, 2)
    other = 1 - c
    z = lax.div(dp, nyh)
    yh = lax.rem(dp, nyh)
    sibling = (dp, 2 * q + other)

    def chip(p):
        return (dp, 2 * p + c)

    def column(zz):
        return (zz * nyh + yh, m)

    def row(yy, mm):
        return (z * nyh + yy, mm)

    def remote(src, dst, send, recv, device):
        return pltpu.make_async_remote_copy(
            src_ref=src, dst_ref=dst, send_sem=send, recv_sem=recv, device_id=device, device_id_type=MESH
        )

    pieces = [(h, k) for h in (other, c) for k in range(np_)]

    def examples(h, k):
        return pl.ds(h * half_e + k * piece_e, piece_e)

    inputs = []
    for i, (h, k) in enumerate(pieces):
        inputs.append(
            (
                pltpu.make_async_copy(x_ref.at[examples(h, k)], x_v.at[examples(h, k)], in_sem.at[0, i]),
                pltpu.make_async_copy(g_ref.at[examples(h, k)], g_v.at[examples(h, k)], in_sem.at[1, i]),
            )
        )
    small = [
        pltpu.make_async_copy(a, b, small_sem.at[i])
        for i, (a, b) in enumerate(
            (
                (rseed_ref, rseed_v),
                (red_ref, red_v),
                (exp_ref, exp_v),
                (len_ref, len_v),
                (val_ref, val_v),
                (wseed_ref, wseed_v),
            )
        )
    ]
    for copy in small[:4]:
        copy.start()
    for pair in inputs:
        for copy in pair:
            copy.start()
    for copy in small[4:]:
        copy.start()

    barrier = pltpu.get_barrier_semaphore()

    def greet(device):
        pl.semaphore_signal(barrier, inc=1, device_id=device, device_id_type=MESH)

    others = [(dy, dm) for dy in range(nyh) for dm in range(nmp) if (dy, dm) != (0, 0)]

    def neighbour(dy, dm):
        return lax.rem(yh + dy, nyh), lax.rem(m + dm, nmp)

    for dy, dm in others:
        greet(row(*neighbour(dy, dm)))
    for j in range(1, nz):
        greet(column(lax.rem(z + j, nz)))

    rpad[...] = jnp.zeros_like(rpad)
    small[0].wait()
    rpad[0:2, 0:k1] = rseed_v[...]
    ranks = lax.broadcasted_iota(jnp.int32, (128, 128), 0)
    left_a = sign_of(rpad[0:1, :], ranks).T[0:k1].astype(BF16)
    left_b = sign_of(rpad[1:2, :], ranks).T[0:k1].astype(BF16)
    small[1].wait()
    small[2].wait()
    p_out = jnp.concatenate(split(dot(left_a, exp_v[...], NT)), axis=0)
    p_in = jnp.concatenate(split(dot(left_b, red_v[...], NN)), axis=0)
    small[3].wait()

    lane_t = lax.broadcasted_iota(jnp.int32, (k1, tokens), 1)

    def sketch(first):
        def body(i, carry):
            e = first + i
            kept = lane_t < len_v[e]
            out = dot(p_out, g_v[e], NT)
            inn = dot(p_in, x_v[e], NT)
            base = pl.multiple_of(e * per, per)
            u[pl.ds(base, k1), :] = jnp.where(kept, out[:k1] + out[k1:], 0.0)
            u[pl.ds(base + k1, k1), :] = jnp.where(kept, inn[:k1] + inn[k1:], 0.0)
            return carry

        return body

    def sketch_piece(i):
        h, k = pieces[i]
        for copy in inputs[i]:
            copy.wait()
        lax.fori_loop(0, piece_e, sketch(h * half_e + k * piece_e), 0)

    def rows_of(h, k):
        return pl.ds(pl.multiple_of(h * half_rows + k * piece_rows, piece_rows), piece_rows)

    def chunk_of(h, k, p):
        return pl.ds(pl.multiple_of(h * half_rows + k * piece_rows + p * chunk, chunk), chunk)

    def lend(k):
        return remote(u.at[rows_of(other, k)], r1.at[k], s1.at[k], d1.at[k], sibling)

    def spread(k, j):
        p = lax.rem(q + j, nq)
        return remote(u.at[chunk_of(c, k, p)], r2.at[k, j - 1], s2.at[k], d2.at[k], chip(p))

    def spread_all(k):
        return remote(r2.at[k], r2.at[k], s2.at[k], d2.at[k], chip(q))

    def borrowed(k, p):
        return u[chunk_of(c, k, p), :] + r1[k, pl.ds(pl.multiple_of(p * chunk, chunk), chunk), :]

    def spread_piece(k):
        lend(k).wait_recv()
        for j in range(1, nq):
            p = lax.rem(q + j, nq)
            u[chunk_of(c, k, p), :] = borrowed(k, p)
            spread(k, j).start()

    steps = nz // 2
    up = column(lax.rem(z + 1, nz))
    down = column(lax.rem(z + nz - 1, nz))

    def ring(step):
        a = lax.rem(z + nz - step, nz)
        b = lax.rem(z + step, nz)
        if step < steps - 1:
            first, second = vf.at[a], vf.at[b]
        else:
            first, second = vf.at[a, pl.ds(0, vl // 2)], vf.at[b, pl.ds(vl // 2, vl // 2)]
        return (
            remote(first, first, sv.at[0, step], dv.at[0, step], up),
            remote(second, second, sv.at[1, step], dv.at[1, step], down),
        )

    def ring_start(step):
        if step < steps:
            for copy in ring(step):
                copy.start()

    def ring_wait(step):
        if step < steps:
            for copy in ring(step):
                copy.wait_recv()

    sketch_piece(0)
    pl.semaphore_wait(barrier, len(others) + nz - 1)
    lend(0).start()
    for k in range(1, np_):
        sketch_piece(k)
        lend(k).start()
    for k in range(np_):
        sketch_piece(np_ + k)
        spread_piece(k)
        if k == 0:
            small[4].wait()
            vf[z] = val_v[...].astype(F32)
            ring_start(0)

    small[5].wait()
    columns = m * width + lax.broadcasted_iota(jnp.int32, (width, wseed_v.shape[1]), 0)
    ra[...] = sign_of(wseed_v[0:1, :], columns).astype(BF16)
    rb[...] = sign_of(wseed_v[1:2, :], columns).astype(BF16)

    def hand_out(k, j):
        part = uf.at[chunk_of(c, k, q)]
        return remote(part, part, s3.at[k, j - 1], d3.at[k, j - 1], chip(lax.rem(q + j, nq)))

    def landed(k, j):
        p = lax.rem(q + nq - j, nq)
        part = uf.at[chunk_of(c, k, p)]
        return remote(part, part, s3.at[k, j - 1], d3.at[k, j - 1], chip(p))

    def pass_on(k, j):
        part = uf.at[chunk_of(c, k, lax.rem(q + nq - j, nq))]
        return remote(part, part, s4.at[k], d4.at[k], sibling)

    def passed(k):
        part = uf.at[rows_of(other, k)]
        return remote(part, part, s4.at[k], d4.at[k], sibling)

    for k in range(np_):
        own = borrowed(k, q)
        spread_all(k).wait_recv()
        for j in range(1, nq):
            own = own + r2[k, j - 1]
        uf[chunk_of(c, k, q), :] = own
        for j in range(1, nq):
            hand_out(k, j).start()
        pass_on(k, 0).start()
        if k == 0:
            ring_wait(0)
            ring_start(1)
    ring_wait(1)
    ring_start(2)

    def project(first):
        def body(i, carry):
            e = first + i
            base = pl.multiple_of(e * per, per)
            a = jnp.concatenate(split(uf[pl.ds(base, k1), :]), axis=0)
            b = jnp.concatenate(split(uf[pl.ds(base + k1, k1), :]), axis=0)
            down_part = dot(a, x_v[e], NN)
            up_part = dot(b, g_v[e], NN)
            at = pl.ds(pl.multiple_of(e * k1, k1), k1)
            high, low = split(down_part[:k1] + down_part[k1:])
            ha[0, at, :] = high
            ha[1, at, :] = low
            high, low = split(up_part[:k1] + up_part[k1:])
            hb[0, at, :] = high
            hb[1, at, :] = low
            return carry

        return body

    def combine(h, k):
        size = piece_e * k1
        at = pl.ds(pl.multiple_of((h * half_e + k * piece_e) * k1, k1), size)
        total = dot(ha[0, at, :], ra[...], NN) + dot(hb[0, at, :], rb[...], NN)
        total = total + (dot(ha[1, at, :], ra[...], NN) + dot(hb[1, at, :], rb[...], NN))
        total = total * scale
        t[0, at, :] = total[:, :128]
        t[1, at, :] = total[:, 128:]

    for k in range(np_):
        for j in range(1, nq):
            landed(k, j).wait_recv()
            pass_on(k, j).start()
        lax.fori_loop(0, piece_e, project(c * half_e + k * piece_e), 0)
        combine(c, k)
        passed(k).wait_recv()
        lax.fori_loop(0, piece_e, project(other * half_e + k * piece_e), 0)
        combine(other, k)
    for a in range(k1):
        cc, qq, al = (a // 2) % 2, a // 4, a % 2
        for side in range(2):
            ts[cc, qq, al * el : (al + 1) * el, side * 128 : (side + 1) * 128] = t[
                side, pl.ds(a, el, stride=k1), :
            ]

    swap = remote(ts.at[other], r3, s5.at[0], d5.at[0], sibling)
    swap.start()
    ring_wait(2)
    ring_start(3)
    swap.wait_recv()

    def scatter(j):
        p = lax.rem(q + j, nq)
        return remote(ts.at[c, p], r4.at[j - 1], s6.at[0], d6.at[0], chip(p))

    scatter_all = remote(r4, r4, s6.at[0], d6.at[0], chip(q))

    for j in range(1, nq):
        p = lax.rem(q + j, nq)
        ts[c, p] += r3[p]
        scatter(j).start()
    total = ts[c, q] + r3[q]

    ring_wait(3)

    def narrow(i, carry):
        vb[pl.ds(pl.multiple_of(i * vl, vl), vl), :] = vf[i].astype(BF16)
        return carry

    lax.fori_loop(0, nz, narrow, 0)
    ones = jnp.ones((16, vf.shape[2]), BF16)
    wide = vb[...].astype(F32)
    high, low = split(wide * wide)
    vq[0] = (dot(ones, high, NT) + dot(ones, low, NT))[0:1]

    def tally(j):
        p = lax.rem(m + j, nmp)
        return remote(vq.at[0], rq.at[j - 1], sq.at[0], dq.at[0], (dp, p))

    tally_all = remote(rq, rq, sq.at[0], dq.at[0], (dp, m))
    for j in range(1, nmp):
        tally(j).start()
    sc[...] = jnp.zeros_like(sc)

    scatter_all.wait_recv()
    for j in range(1, nq):
        total = total + r4[j - 1]
    tg[yh] = total

    def share(j):
        part = tg.at[yh]
        return remote(part, part, s7.at[0], d7.at[0], row(lax.rem(yh + j, nyh), m))

    shared = remote(tg.at[pl.ds(0, nyh - 1)], tg.at[pl.ds(0, nyh - 1)], s7.at[0], d7.at[0], row(yh, m))
    for j in range(1, nyh):
        share(j).start()
    tp_ref[:, 0:256] = total[0:el]
    tp_ref[:, 256:512] = total[el:te]
    if nyh > 1:
        shared.wait_recv()

    for y in range(nyh):
        for al in range(2):
            lt[y * el : (y + 1) * el, al * 256 : (al + 1) * 256] = tg[y, al * el : (al + 1) * el, :]
    train = lt[...]
    high, low = split(train)
    scores = dot(high, vb[...], NT) + dot(low, vb[...], NT)
    high, low = split(train * train)
    squares = (dot(ones, high, NT) + dot(ones, low, NT))[0:1]
    rows = nyh * el
    for i in range(nmp):
        sc[i, 0:er, :] = scores[i * er : (i + 1) * er, 0:hv]
        sc[i, er : 2 * er, :] = scores[i * er : (i + 1) * er, hv : 2 * hv]
        sc[i, 2 * er : 2 * er + 1, 0:rows] = squares

    def deal(j):
        p = lax.rem(m + j, nmp)
        return remote(sc.at[p], r5.at[j - 1], s8.at[0], d8.at[0], (dp, p))

    deal_all = remote(r5, r5, s8.at[0], d8.at[0], (dp, m))
    for j in range(1, nmp):
        deal(j).start()
    tally_all.wait_recv()
    norms = vq[0]
    for j in range(1, nmp):
        norms = norms + rq[j - 1]
    norms = lax.rsqrt(norms + EPSILON)
    row_id = lax.broadcasted_iota(jnp.int32, (8, hv), 0)
    lane_id = lax.broadcasted_iota(jnp.int32, (8, hv), 1)
    norms = jnp.where(row_id < er, norms[:, 0:hv], norms[:, hv : 2 * hv])
    deal_all.wait_recv()
    summed = sc[m]
    for j in range(1, nmp):
        summed = summed + r5[j - 1]

    cosines = summed * norms
    e_of = jnp.where(row_id < er, row_id, row_id - er)
    squares = jnp.sum(
        jnp.where(lane_id == m * er + e_of, summed[2 * er : 2 * er + 1, :], 0.0), axis=1, keepdims=True
    )
    weight = lax.rsqrt(squares + EPSILON) * root_k
    row_o = lax.broadcasted_iota(jnp.int32, (8, 128), 0)
    lane_o = lax.broadcasted_iota(jnp.int32, (8, 128), 1)
    placed = jnp.full((8, 128), LOWEST, F32)
    first_half = row_o < er
    e_of = jnp.where(first_half, row_o, row_o - er)
    for g in range(nz // 2):
        here = (lane_id >= g * vl) & (lane_id < (g + 1) * vl)
        best = jnp.max(jnp.where(here, cosines, LOWEST), axis=1, keepdims=True) * weight
        lane = e_of * nz + jnp.where(first_half, 0, nz // 2) + g
        placed = jnp.where((lane_o == lane) & (row_o < 2 * er), best, placed)
    mine = yh * nmp + m
    fp[mine] = jnp.max(placed, axis=0, keepdims=True)

    def tell(dy, dm):
        part = fp.at[mine]
        return remote(part, part, s9.at[0], d9.at[0], row(*neighbour(dy, dm)))

    told = remote(fp.at[pl.ds(0, len(others))], fp.at[pl.ds(0, len(others))], s9.at[0], d9.at[0], row(yh, m))
    for dy, dm in others:
        tell(dy, dm).start()
    told.wait_recv()
    best = fp[0:nmp]
    for y in range(1, nyh):
        best = jnp.maximum(best, fp[y * nmp : (y + 1) * nmp])
    fz[z] = best

    def publish(j):
        part = fz.at[z]
        return remote(part, part, s10.at[0], d10.at[0], column(lax.rem(z + j, nz)))

    published = remote(fz.at[pl.ds(0, nz - 1)], fz.at[pl.ds(0, nz - 1)], s10.at[0], d10.at[0], column(z))
    for j in range(1, nz):
        publish(j).start()

    for k in range(np_):
        lend(k).wait_send()
        spread_all(k).wait_send()
        passed(k).wait_send()
        for j in range(1, nq):
            hand_out(k, j).wait_send()
    swap.wait_send()
    scatter_all.wait_send()
    for step in range(steps):
        for copy in ring(step):
            copy.wait_send()
    tally_all.wait_send()
    if nyh > 1:
        shared.wait_send()
    deal_all.wait_send()
    told.wait_send()
    published.wait_recv()
    inf_ref[...] = fz[...]
    published.wait_send()


def on_device(nz, nyh, nq, np_, scale, root_k, *args):
    inputs, _, lengths, reducing, expanding, wseeds, rseeds, validation = args
    el, tokens, width = inputs.shape
    nmp = 2 * nq
    k1 = 2 * nmp
    vl, kl = validation.shape
    k2 = wseeds.shape[1]
    half_rows = el * k1
    piece_rows = half_rows // np_
    chunk = piece_rows // nq
    hv = nz * vl // 2
    dma = pltpu.SemaphoreType.DMA
    scratch = [
        pltpu.VMEM(inputs.shape, BF16),
        pltpu.VMEM(inputs.shape, BF16),
        pltpu.SMEM(lengths.shape, jnp.int32),
        pltpu.VMEM(reducing.shape, BF16),
        pltpu.VMEM(expanding.shape, BF16),
        pltpu.VMEM(wseeds.shape, jnp.int32),
        pltpu.VMEM(rseeds.shape, jnp.int32),
        pltpu.VMEM((8, 128), jnp.int32),
        pltpu.VMEM(validation.shape, BF16),
        pltpu.VMEM((2 * half_rows, tokens), F32),
        pltpu.VMEM((np_, piece_rows, tokens), F32),
        pltpu.VMEM((np_, nq - 1, chunk, tokens), F32),
        pltpu.VMEM((2 * half_rows, tokens), F32),
        pltpu.VMEM((width, k2), BF16),
        pltpu.VMEM((width, k2), BF16),
        pltpu.VMEM((2, el * k1, width), BF16),
        pltpu.VMEM((2, el * k1, width), BF16),
        pltpu.VMEM((2, el * k1, 128), F32),
        pltpu.VMEM((2, nq, 2 * el, k2), F32),
        pltpu.VMEM((nq, 2 * el, k2), F32),
        pltpu.VMEM((nq - 1, 2 * el, k2), F32),
        pltpu.VMEM((nyh, 2 * el, k2), F32),
        pltpu.VMEM((nyh * el, kl), F32),
        pltpu.VMEM((nz, vl, kl), F32),
        pltpu.VMEM((nz * vl, kl), BF16),
        pltpu.VMEM((1, 1, nz * vl), F32),
        pltpu.VMEM((nmp - 1, 1, nz * vl), F32),
        pltpu.VMEM((nmp, 8, hv), F32),
        pltpu.VMEM((nmp - 1, 8, hv), F32),
        pltpu.VMEM((nyh * nmp, 1, 128), F32),
        pltpu.VMEM((nz, nmp, 1, 128), F32),
        dma((2, 2 * np_)),
        dma((6,)),
    ]
    one = (1,)
    for count in (
        (np_,),
        (np_,),
        (np_, nq - 1),
        (np_,),
        one,
        one,
        one,
        (2, nz // 2),
        one,
        one,
        one,
        one,
    ):
        scratch += [dma(count), dma(count)]
    train_proj, best = pl.pallas_call(
        functools.partial(kernel, nz, nyh, nq, np_, scale, root_k),
        out_shape=(
            jax.ShapeDtypeStruct((el, kl), F32),
            jax.ShapeDtypeStruct((nz, nmp, 1, 128), F32),
        ),
        in_specs=[pl.BlockSpec(memory_space=pltpu.HBM)] * len(args),
        out_specs=[pl.BlockSpec(memory_space=pltpu.VMEM)] * 2,
        scratch_shapes=scratch,
        compiler_params=pltpu.CompilerParams(
            collective_id=0, has_side_effects=True, vmem_limit_bytes=48 * 1024 * 1024
        ),
    )(*[pltpu.with_memory_space_constraint(a, pltpu.HBM) for a in args])
    er = nyh * el // nmp
    influence = best.reshape(nz * nmp, 128)[:, : er * nz].reshape(nz * nmp * er, nz)
    return (train_proj, influence)


def solution(mesh, nyh=4, np_=2):
    ndp, nmp = mesh.shape["dp"], mesh.shape["mp"]
    nz, nq = ndp // nyh, nmp // 2
    width = nmp * 256
    scale = 1.0 / math.sqrt(2.0 * 128 * width * 256)
    root_k = math.sqrt(2 * nmp * 256)
    in_specs = (
        P("dp", None, "mp"),
        P("dp", None, "mp"),
        P("dp"),
        P(None, "mp"),
        P("mp", None),
        P(),
        P(),
        P("dp", "mp"),
    )
    return jax.shard_map(
        functools.partial(on_device, nz, nyh, nq, np_, scale, root_k),
        mesh=mesh,
        in_specs=in_specs,
        out_specs=(P("dp", "mp"), P()),
        check_vma=False,
    )
```

time: 79.9 us -> 62 us (0.78)
  Pallas kernels: 70.2 us -> 59.8 us
  local copies, waits for them, and re-layouts: 8.76 us -> 1.42 us
    pallas_call x1, Pallas kernels: 70.2 us -> 59.8 us  [on_device(): pl.pallas_call(functools.partial(kernel, nz, nyh, nq, np_, scale, root_k)...]
    unnamed x18 -> x2, local copies, waits for them, and re-layouts: 8.66 us -> 1.32 us
where the time goes in v2:
time: 62 us; the launch traced here: 61.8 us
  Pallas kernels  59.8 us (96%)
  local copies, waits for them, and re-layouts  1.42 us (2%)
  between operations  0.65 us (1%)
    pallas_call x1, Pallas kernels, on_device(): pl.pallas_call(functools.partial(kernel, nz, nyh, nq, np_, scale, root_k)...  59.8 us
    unnamed x2, local copies, waits for them, and re-layouts  1.32 us

profile of v2, /device:TPU:1, one launch (start us, length us, event | category | flops | bytes accessed | tf_op | source)
XLA Modules:
  0.0 61.8 jit_solution(2427956574455513482)
XLA Ops:
  0.6 59.8 %shard_map.95 = (f32[12,512]{1,0:T(8,128)S(1)}, f32[8,16,1,128]{3,2,1,0:T(1,128)S(1)}) custom-call(bf16[12,256,256]{2,1,0:T(8,128)(2,1)} %refs_0_.1, bf16[12,256,256]{2,1,0:T(8,128)(2,1)} %refs_1_.1, s32[12]{0:T(128)} %refs_2_.1, bf16[128,256]{1,0:T(8,128)(2,1)} %refs_3_.1, bf16[256,128]{1,0:T(8,128)(2,1)} %refs_4_.1, s32[2,256]{1,0:T(2,128)} %refs_5_.1, ...), custom_call_target="tpu_custom_call" | custom-call | tf_op jit(solution)/shard_map/pallas_call | solution.py:530
  60.4 0.1 reshape.11
  60.5 0.7 %copy.10 = f32[384,8]{0,1:T(8,128)} copy(f32[384,8]{1,0:T(8,128)S(1)} %reshape.11) | data formatting | bytes 24576
  61.2 0.6 copy.12

commit v3 on v2

--- a/solution.py
+++ b/solution.py
@@ -43,7 +43,7 @@
         (x_ref, g_ref, len_ref, red_ref, exp_ref, wseed_ref, rseed_ref, val_ref, tp_ref, inf_ref),
         (x_v, g_v, len_v, red_v, exp_v, wseed_v, rseed_v, rpad, val_v, u, r1, r2, uf, ra, rb, ha, hb, t, ts, r3, r4),
         (tg, lt, vf, vb, vq, rq, sc, r5, fp, fz),
-        (in_sem, small_sem, s1, d1, s2, d2, s3, d3, s4, d4, s5, d5, s6, d6, s7, d7, sv, dv, sq, dq, s8, d8, s9, d9, s10, d10),
+        (in_sem, small_sem, s1, d1, s2, d2, s3, d3, s4, d4, s5, d5, s6, d6, s7, d7, sv, dv, sq, dq, s8, d8, s9, d9, s10, d10, near),
     ) = refs[:10], refs[10:31], refs[31:41], refs[41:]
     nmp = 2 * nq
     el = x_v.shape[0]
@@ -69,6 +69,26 @@
     z = lax.div(dp, nyh)
     yh = lax.rem(dp, nyh)
     sibling = (dp, 2 * q + other)
+
+    nx = nq // 2
+    ylo = lax.div(q, nx)
+    x = lax.rem(q, nx)
+
+    def ring_hops(d, n):
+        return min(d, n - d)
+
+    chips = [(dy, dx) for dy in range(2) for dx in range(nx) if (dy, dx) != (0, 0)]
+    chips.sort(key=lambda d: -(d[0] + ring_hops(d[1], nx)))
+    group = [(dy, dx, dc) for dy in range(2) for dx in range(nx) for dc in range(2) if (dy, dx, dc) != (0, 0, 0)]
+    group.sort(key=lambda d: -(d[0] + ring_hops(d[1], nx)))
+    planes = sorted(range(1, nz), key=lambda d: -ring_hops(d, nz))
+    lines = sorted(range(1, nyh), key=lambda d: -ring_hops(d, nyh))
+
+    def chip_at(shift, sign=1):
+        return lax.rem(ylo + shift[0], 2) * nx + lax.rem(x + nx + sign * shift[1], nx)
+
+    def member(shift):
+        return 2 * chip_at(shift) + lax.rem(c + shift[2], 2)
 
     def chip(p):
         return (dp, 2 * p + c)
@@ -110,28 +130,26 @@
             )
         )
     ]
-    for copy in small[:4]:
+    for copy in small[:3] + list(inputs[0]):
         copy.start()
-    for pair in inputs:
-        for copy in pair:
-            copy.start()
-    for copy in small[4:]:
+
+    barrier = pltpu.get_barrier_semaphore()
+    shifts = (2, -2, 1, -1) if nz == 8 else (1, -1)
+    sides = [j for j in (1, nyh - 1) if j < nyh][: nyh - 1]
+    sides = sides[:1] if nyh == 2 else sides
+    near_by = [sibling] + [chip(chip_at(shift)) for shift in chips]
+    near_by += [column(lax.rem(z + nz + d, nz)) for d in shifts]
+    near_by += [row(lax.rem(yh + j, nyh), m) for j in sides]
+    for device in near_by:
+        pl.semaphore_signal(barrier, inc=1, device_id=device, device_id_type=MESH)
+    for copy in [small[3]] + [copy for pair in inputs[1:] for copy in pair] + small[4:]:
         copy.start()
 
-    barrier = pltpu.get_barrier_semaphore()
-
-    def greet(device):
-        pl.semaphore_signal(barrier, inc=1, device_id=device, device_id_type=MESH)
-
-    others = [(dy, dm) for dy in range(nyh) for dm in range(nmp) if (dy, dm) != (0, 0)]
-
-    def neighbour(dy, dm):
-        return lax.rem(yh + dy, nyh), lax.rem(m + dm, nmp)
-
-    for dy, dm in others:
-        greet(row(*neighbour(dy, dm)))
-    for j in range(1, nz):
-        greet(column(lax.rem(z + j, nz)))
+    others = [(dyh, *shift) for dyh in range(nyh) for shift in [(0, 0, 0)] + group if (dyh, *shift) != (0, 0, 0, 0)]
+    others.sort(key=lambda d: -(2 * ring_hops(d[0], nyh) + d[1] + ring_hops(d[2], nx)))
+
+    def neighbour(dyh, *shift):
+        return lax.rem(yh + dyh, nyh), member(shift)
 
     rpad[...] = jnp.zeros_like(rpad)
     small[0].wait()
@@ -175,9 +193,9 @@
     def lend(k):
         return remote(u.at[rows_of(other, k)], r1.at[k], s1.at[k], d1.at[k], sibling)
 
-    def spread(k, j):
-        p = lax.rem(q + j, nq)
-        return remote(u.at[chunk_of(c, k, p)], r2.at[k, j - 1], s2.at[k], d2.at[k], chip(p))
+    def spread(k, i):
+        p = chip_at(chips[i])
+        return remote(u.at[chunk_of(c, k, p)], r2.at[k, i], s2.at[k], d2.at[k], chip(p))
 
     def spread_all(k):
         return remote(r2.at[k], r2.at[k], s2.at[k], d2.at[k], chip(q))
@@ -187,67 +205,61 @@
 
     def spread_piece(k):
         lend(k).wait_recv()
-        for j in range(1, nq):
-            p = lax.rem(q + j, nq)
+        for i, shift in enumerate(chips):
+            p = chip_at(shift)
             u[chunk_of(c, k, p), :] = borrowed(k, p)
-            spread(k, j).start()
-
-    steps = nz // 2
-    up = column(lax.rem(z + 1, nz))
-    down = column(lax.rem(z + nz - 1, nz))
-
-    def ring(step):
-        a = lax.rem(z + nz - step, nz)
-        b = lax.rem(z + step, nz)
-        if step < steps - 1:
-            first, second = vf.at[a], vf.at[b]
-        else:
-            first, second = vf.at[a, pl.ds(0, vl // 2)], vf.at[b, pl.ds(vl // 2, vl // 2)]
-        return (
-            remote(first, first, sv.at[0, step], dv.at[0, step], up),
-            remote(second, second, sv.at[1, step], dv.at[1, step], down),
-        )
-
-    def ring_start(step):
-        if step < steps:
-            for copy in ring(step):
-                copy.start()
-
-    def ring_wait(step):
-        if step < steps:
-            for copy in ring(step):
-                copy.wait_recv()
-
-    sketch_piece(0)
-    pl.semaphore_wait(barrier, len(others) + nz - 1)
-    lend(0).start()
-    for k in range(1, np_):
+            spread(k, i).start()
+
+    def along(i, offset, shift, part):
+        at = lax.rem(z + nz + offset, nz)
+        block = vf.at[at] if part is None else vf.at[at, pl.ds(part * (vl // 2), vl // 2)]
+        return remote(block, block, sv.at[i], dv.at[i], column(lax.rem(z + nz + shift, nz)))
+
+    def arrival(i, offset, shift, part):
+        at = lax.rem(z + 2 * nz + offset - shift, nz)
+        block = vf.at[at] if part is None else vf.at[at, pl.ds(part * (vl // 2), vl // 2)]
+        return remote(block, block, sv.at[i], dv.at[i], column(lax.rem(z + nz - shift, nz)))
+
+    first_hop = [(i, 0, d, None) for i, d in enumerate(shifts)]
+    if nz == 8:
+        second_hop = [(4, -2, 1, None), (5, 2, -1, None), (6, -2, 2, 0), (7, 2, -2, 1)]
+    else:
+        second_hop = [(2, -1, 1, 0), (3, 1, -1, 1)]
+
+    early = min(np_, 2)
+    for k in range(early):
         sketch_piece(k)
+    pl.semaphore_wait(barrier, len(near_by))
+    for k in range(np_):
+        if k >= early:
+            sketch_piece(k)
         lend(k).start()
+    for j in sides:
+        pl.semaphore_signal(near, inc=1, device_id=row(lax.rem(yh + j, nyh), m), device_id_type=MESH)
+    small[4].wait()
+    vf[z] = val_v[...].astype(F32)
+    for hop in first_hop:
+        along(*hop).start()
     for k in range(np_):
         sketch_piece(np_ + k)
         spread_piece(k)
-        if k == 0:
-            small[4].wait()
-            vf[z] = val_v[...].astype(F32)
-            ring_start(0)
 
     small[5].wait()
     columns = m * width + lax.broadcasted_iota(jnp.int32, (width, wseed_v.shape[1]), 0)
     ra[...] = sign_of(wseed_v[0:1, :], columns).astype(BF16)
     rb[...] = sign_of(wseed_v[1:2, :], columns).astype(BF16)
 
-    def hand_out(k, j):
+    def hand_out(k, i):
         part = uf.at[chunk_of(c, k, q)]
-        return remote(part, part, s3.at[k, j - 1], d3.at[k, j - 1], chip(lax.rem(q + j, nq)))
-
-    def landed(k, j):
-        p = lax.rem(q + nq - j, nq)
+        return remote(part, part, s3.at[k, i], d3.at[k, i], chip(chip_at(chips[i])))
+
+    def landed(k, i):
+        p = chip_at(chips[i], -1)
         part = uf.at[chunk_of(c, k, p)]
-        return remote(part, part, s3.at[k, j - 1], d3.at[k, j - 1], chip(p))
-
-    def pass_on(k, j):
-        part = uf.at[chunk_of(c, k, lax.rem(q + nq - j, nq))]
+        return remote(part, part, s3.at[k, i], d3.at[k, i], chip(p))
+
+    def pass_on(k, p):
+        part = uf.at[chunk_of(c, k, p)]
         return remote(part, part, s4.at[k], d4.at[k], sibling)
 
     def passed(k):
@@ -260,14 +272,15 @@
         for j in range(1, nq):
             own = own + r2[k, j - 1]
         uf[chunk_of(c, k, q), :] = own
-        for j in range(1, nq):
-            hand_out(k, j).start()
-        pass_on(k, 0).start()
-        if k == 0:
-            ring_wait(0)
-            ring_start(1)
-    ring_wait(1)
-    ring_start(2)
+        for i in range(len(chips)):
+            hand_out(k, i).start()
+        pass_on(k, q).start()
+
+    def ring_on():
+        for hop in first_hop[:2]:
+            arrival(*hop).wait_recv()
+        for hop in second_hop:
+            along(*hop).start()
 
     def project(first):
         def body(i, carry):
@@ -297,15 +310,25 @@
         t[0, at, :] = total[:, :128]
         t[1, at, :] = total[:, 128:]
 
-    for k in range(np_):
-        for j in range(1, nq):
-            landed(k, j).wait_recv()
-            pass_on(k, j).start()
-        lax.fori_loop(0, piece_e, project(c * half_e + k * piece_e), 0)
-        combine(c, k)
-        passed(k).wait_recv()
-        lax.fori_loop(0, piece_e, project(other * half_e + k * piece_e), 0)
-        combine(other, k)
+    def arrive(k):
+        for i in reversed(range(len(chips))):
+            landed(k, i).wait_recv()
+            pass_on(k, chip_at(chips[i], -1)).start()
+
+    def project_piece(h, k):
+        lax.fori_loop(0, piece_e, project(h * half_e + k * piece_e), 0)
+        combine(h, k)
+
+    arrive(0)
+    project_piece(c, 0)
+    ring_on()
+    for k in range(1, np_):
+        arrive(k)
+        passed(k - 1).wait_recv()
+        project_piece(other, k - 1)
+        project_piece(c, k)
+    passed(np_ - 1).wait_recv()
+    project_piece(other, np_ - 1)
     for a in range(k1):
         cc, qq, al = (a // 2) % 2, a // 4, a % 2
         for side in range(2):
@@ -315,23 +338,22 @@
 
     swap = remote(ts.at[other], r3, s5.at[0], d5.at[0], sibling)
     swap.start()
-    ring_wait(2)
-    ring_start(3)
     swap.wait_recv()
 
-    def scatter(j):
-        p = lax.rem(q + j, nq)
-        return remote(ts.at[c, p], r4.at[j - 1], s6.at[0], d6.at[0], chip(p))
+    def scatter(i):
+        p = chip_at(chips[i])
+        return remote(ts.at[c, p], r4.at[i], s6.at[0], d6.at[0], chip(p))
 
     scatter_all = remote(r4, r4, s6.at[0], d6.at[0], chip(q))
 
-    for j in range(1, nq):
-        p = lax.rem(q + j, nq)
+    for i, shift in enumerate(chips):
+        p = chip_at(shift)
         ts[c, p] += r3[p]
-        scatter(j).start()
+        scatter(i).start()
     total = ts[c, q] + r3[q]
 
-    ring_wait(3)
+    for hop in first_hop[2:] + second_hop:
+        arrival(*hop).wait_recv()
 
     def narrow(i, carry):
         vb[pl.ds(pl.multiple_of(i * vl, vl), vl), :] = vf[i].astype(BF16)
@@ -343,13 +365,12 @@
     high, low = split(wide * wide)
     vq[0] = (dot(ones, high, NT) + dot(ones, low, NT))[0:1]
 
-    def tally(j):
-        p = lax.rem(m + j, nmp)
-        return remote(vq.at[0], rq.at[j - 1], sq.at[0], dq.at[0], (dp, p))
+    def tally(i):
+        return remote(vq.at[0], rq.at[i], sq.at[0], dq.at[0], (dp, member(group[i])))
 
     tally_all = remote(rq, rq, sq.at[0], dq.at[0], (dp, m))
-    for j in range(1, nmp):
-        tally(j).start()
+    for i in range(len(group)):
+        tally(i).start()
     sc[...] = jnp.zeros_like(sc)
 
     scatter_all.wait_recv()
@@ -362,7 +383,9 @@
         return remote(part, part, s7.at[0], d7.at[0], row(lax.rem(yh + j, nyh), m))
 
     shared = remote(tg.at[pl.ds(0, nyh - 1)], tg.at[pl.ds(0, nyh - 1)], s7.at[0], d7.at[0], row(yh, m))
-    for j in range(1, nyh):
+    if sides:
+        pl.semaphore_wait(near, len(sides))
+    for j in lines:
         share(j).start()
     tp_ref[:, 0:256] = total[0:el]
     tp_ref[:, 256:512] = total[el:te]
@@ -383,13 +406,13 @@
         sc[i, er : 2 * er, :] = scores[i * er : (i + 1) * er, hv : 2 * hv]
         sc[i, 2 * er : 2 * er + 1, 0:rows] = squares
 
-    def deal(j):
-        p = lax.rem(m + j, nmp)
-        return remote(sc.at[p], r5.at[j - 1], s8.at[0], d8.at[0], (dp, p))
+    def deal(i):
+        p = member(group[i])
+        return remote(sc.at[p], r5.at[i], s8.at[0], d8.at[0], (dp, p))
 
     deal_all = remote(r5, r5, s8.at[0], d8.at[0], (dp, m))
-    for j in range(1, nmp):
-        deal(j).start()
+    for i in range(len(group)):
+        deal(i).start()
     tally_all.wait_recv()
     norms = vq[0]
     for j in range(1, nmp):
@@ -422,13 +445,13 @@
     mine = yh * nmp + m
     fp[mine] = jnp.max(placed, axis=0, keepdims=True)
 
-    def tell(dy, dm):
+    def tell(shift):
         part = fp.at[mine]
-        return remote(part, part, s9.at[0], d9.at[0], row(*neighbour(dy, dm)))
+        return remote(part, part, s9.at[0], d9.at[0], row(*neighbour(*shift)))
 
     told = remote(fp.at[pl.ds(0, len(others))], fp.at[pl.ds(0, len(others))], s9.at[0], d9.at[0], row(yh, m))
-    for dy, dm in others:
-        tell(dy, dm).start()
+    for shift in others:
+        tell(shift).start()
     told.wait_recv()
     best = fp[0:nmp]
     for y in range(1, nyh):
@@ -440,20 +463,19 @@
         return remote(part, part, s10.at[0], d10.at[0], column(lax.rem(z + j, nz)))
 
     published = remote(fz.at[pl.ds(0, nz - 1)], fz.at[pl.ds(0, nz - 1)], s10.at[0], d10.at[0], column(z))
-    for j in range(1, nz):
+    for j in planes:
         publish(j).start()
 
     for k in range(np_):
         lend(k).wait_send()
         spread_all(k).wait_send()
         passed(k).wait_send()
-        for j in range(1, nq):
-            hand_out(k, j).wait_send()
+        for i in range(len(chips)):
+            hand_out(k, i).wait_send()
     swap.wait_send()
     scatter_all.wait_send()
-    for step in range(steps):
-        for copy in ring(step):
-            copy.wait_send()
+    for hop in first_hop + second_hop:
+        along(*hop).wait_send()
     tally_all.wait_send()
     if nyh > 1:
         shared.wait_send()
@@ -520,13 +542,14 @@
         one,
         one,
         one,
-        (2, nz // 2),
+        (nz,),
         one,
         one,
         one,
         one,
     ):
         scratch += [dma(count), dma(count)]
+    scratch.append(pltpu.SemaphoreType.REGULAR)
     train_proj, best = pl.pallas_call(
         functools.partial(kernel, nz, nyh, nq, np_, scale, root_k),
         out_shape=(

time: 62 us -> 57.1 us (0.921)
  Pallas kernels: 59.8 us -> 54.9 us
    pallas_call x1, Pallas kernels: 59.8 us -> 54.9 us  [on_device(): pl.pallas_call(functools.partial(kernel, nz, nyh, nq, np_, scale, root_k)...]
where the time goes in v3:
time: 57.1 us; the launch traced here: 57 us
  Pallas kernels  54.9 us (96%)
  local copies, waits for them, and re-layouts  1.42 us (2%)
  between operations  0.65 us (1%)
    pallas_call x1, Pallas kernels, on_device(): pl.pallas_call(functools.partial(kernel, nz, nyh, nq, np_, scale, root_k)...  54.9 us
    unnamed x2, local copies, waits for them, and re-layouts  1.32 us

profile of v3, /device:TPU:1, one launch (start us, length us, event | category | flops | bytes accessed | tf_op | source)
XLA Modules:
  0.0 57.0 jit_solution(687660620671812227)
XLA Ops:
  0.6 54.9 %shard_map.95 = (f32[12,512]{1,0:T(8,128)S(1)}, f32[8,16,1,128]{3,2,1,0:T(1,128)S(1)}) custom-call(bf16[12,256,256]{2,1,0:T(8,128)(2,1)} %refs_0_.1, bf16[12,256,256]{2,1,0:T(8,128)(2,1)} %refs_1_.1, s32[12]{0:T(128)} %refs_2_.1, bf16[128,256]{1,0:T(8,128)(2,1)} %refs_3_.1, bf16[256,128]{1,0:T(8,128)(2,1)} %refs_4_.1, s32[2,256]{1,0:T(2,128)} %refs_5_.1, ...), custom_call_target="tpu_custom_call" | custom-call | tf_op jit(solution)/shard_map/pallas_call | solution.py:553
  55.6 0.1 reshape.11
  55.7 0.7 %copy.10 = f32[384,8]{0,1:T(8,128)} copy(f32[384,8]{1,0:T(8,128)S(1)} %reshape.11) | data formatting | bytes 24576
  56.4 0.6 %copy.12 = f32[12,512]{1,0:T(8,128)} copy(f32[12,512]{1,0:T(8,128)S(1)} %get-tuple-element.10) | data formatting | bytes 49152

commit v4 on v3

--- a/solution.py
+++ b/solution.py
@@ -41,10 +41,10 @@
 def kernel(nz, nyh, nq, np_, scale, root_k, *refs):
     (
         (x_ref, g_ref, len_ref, red_ref, exp_ref, wseed_ref, rseed_ref, val_ref, tp_ref, inf_ref),
-        (x_v, g_v, len_v, red_v, exp_v, wseed_v, rseed_v, rpad, val_v, u, r1, r2, uf, ra, rb, ha, hb, t, ts, r3, r4),
+        (x_v, g_v, len_v, red_v, exp_v, wseed_v, rseed_v, rpad, val_v, u, r1, r2, uf, ra, rb, ha, hb, t, ts, r4, xf, xr, xs),
         (tg, lt, vf, vb, vq, rq, sc, r5, fp, fz),
-        (in_sem, small_sem, s1, d1, s2, d2, s3, d3, s4, d4, s5, d5, s6, d6, s7, d7, sv, dv, sq, dq, s8, d8, s9, d9, s10, d10, near),
-    ) = refs[:10], refs[10:31], refs[31:41], refs[41:]
+        (in_sem, small_sem, s1, d1, s2, d2, s3, d3, s4, d4, s6, d6, s7, d7, sv, dv, sq, dq, s8, d8, s9, d9, s10, d10, near),
+    ) = refs[:10], refs[10:33], refs[33:43], refs[43:]
     nmp = 2 * nq
     el = x_v.shape[0]
     k1 = nmp * 2
@@ -182,7 +182,7 @@
         h, k = pieces[i]
         for copy in inputs[i]:
             copy.wait()
-        lax.fori_loop(0, piece_e, sketch(h * half_e + k * piece_e), 0)
+        lax.fori_loop(0, piece_e, sketch(h * half_e + k * piece_e), 0, unroll=True)
 
     def rows_of(h, k):
         return pl.ds(pl.multiple_of(h * half_rows + k * piece_rows, piece_rows), piece_rows)
@@ -226,13 +226,10 @@
     else:
         second_hop = [(2, -1, 1, 0), (3, 1, -1, 1)]
 
-    early = min(np_, 2)
-    for k in range(early):
+    for k in range(np_ + 1):
         sketch_piece(k)
     pl.semaphore_wait(barrier, len(near_by))
     for k in range(np_):
-        if k >= early:
-            sketch_piece(k)
         lend(k).start()
     for j in sides:
         pl.semaphore_signal(near, inc=1, device_id=row(lax.rem(yh + j, nyh), m), device_id_type=MESH)
@@ -241,40 +238,45 @@
     for hop in first_hop:
         along(*hop).start()
     for k in range(np_):
-        sketch_piece(np_ + k)
+        if k:
+            sketch_piece(np_ + k)
         spread_piece(k)
 
+    def trade(k, side):
+        part = pl.ds(k * piece_e, piece_e)
+        return remote(xf.at[side, part], xr.at[side, part], s4.at[k, side], d4.at[k, side], sibling)
+
+    for k in range(np_):
+        for side, tokens_v in enumerate((x_v, g_v)):
+
+            def widen(i, carry, side=side, tokens_v=tokens_v, k=k):
+                xf[side, k * piece_e + i] = tokens_v[other * half_e + k * piece_e + i].astype(F32)
+                return carry
+
+            lax.fori_loop(0, piece_e, widen, 0)
+            trade(k, side).start()
+
     small[5].wait()
-    columns = m * width + lax.broadcasted_iota(jnp.int32, (width, wseed_v.shape[1]), 0)
-    ra[...] = sign_of(wseed_v[0:1, :], columns).astype(BF16)
-    rb[...] = sign_of(wseed_v[1:2, :], columns).astype(BF16)
+    for s, device in enumerate((m, 2 * q + other)):
+        columns = device * width + lax.broadcasted_iota(jnp.int32, (width, wseed_v.shape[1]), 0)
+        ra[s] = sign_of(wseed_v[0:1, :], columns).astype(BF16)
+        rb[s] = sign_of(wseed_v[1:2, :], columns).astype(BF16)
 
     def hand_out(k, i):
-        part = uf.at[chunk_of(c, k, q)]
-        return remote(part, part, s3.at[k, i], d3.at[k, i], chip(chip_at(chips[i])))
-
-    def landed(k, i):
-        p = chip_at(chips[i], -1)
-        part = uf.at[chunk_of(c, k, p)]
-        return remote(part, part, s3.at[k, i], d3.at[k, i], chip(p))
-
-    def pass_on(k, p):
-        part = uf.at[chunk_of(c, k, p)]
-        return remote(part, part, s4.at[k], d4.at[k], sibling)
-
-    def passed(k):
-        part = uf.at[rows_of(other, k)]
-        return remote(part, part, s4.at[k], d4.at[k], sibling)
+        part = uf.at[chunk_of(0, k, q)]
+        return remote(part, part, s3.at[k], d3.at[k], chip(chip_at(chips[i])))
+
+    def landed(k):
+        return remote(r2.at[k], r2.at[k], s3.at[k], d3.at[k], chip(q))
 
     for k in range(np_):
         own = borrowed(k, q)
         spread_all(k).wait_recv()
         for j in range(1, nq):
             own = own + r2[k, j - 1]
-        uf[chunk_of(c, k, q), :] = own
+        uf[chunk_of(0, k, q), :] = own
         for i in range(len(chips)):
             hand_out(k, i).start()
-        pass_on(k, q).start()
 
     def ring_on():
         for hop in first_hop[:2]:
@@ -282,75 +284,61 @@
         for hop in second_hop:
             along(*hop).start()
 
-    def project(first):
-        def body(i, carry):
-            e = first + i
-            base = pl.multiple_of(e * per, per)
-            a = jnp.concatenate(split(uf[pl.ds(base, k1), :]), axis=0)
-            b = jnp.concatenate(split(uf[pl.ds(base + k1, k1), :]), axis=0)
-            down_part = dot(a, x_v[e], NN)
-            up_part = dot(b, g_v[e], NN)
-            at = pl.ds(pl.multiple_of(e * k1, k1), k1)
-            high, low = split(down_part[:k1] + down_part[k1:])
-            ha[0, at, :] = high
-            ha[1, at, :] = low
-            high, low = split(up_part[:k1] + up_part[k1:])
-            hb[0, at, :] = high
-            hb[1, at, :] = low
-            return carry
-
-        return body
-
-    def combine(h, k):
+    for k in range(np_):
+        for side in range(2):
+            trade(k, side).wait_recv()
+
+            def narrow_tokens(i, carry, side=side, k=k):
+                xs[side, k * piece_e + i] = xr[side, k * piece_e + i].astype(BF16)
+                return carry
+
+            lax.fori_loop(0, piece_e, narrow_tokens, 0)
+    ring_on()
+
+    def project(i, carry):
+        base = i * per
+        a = jnp.concatenate(split(uf[pl.ds(base, k1), :]), axis=0)
+        b = jnp.concatenate(split(uf[pl.ds(base + k1, k1), :]), axis=0)
+        at = pl.ds(i * k1, k1)
+        e = c * half_e + i
+        for s, (xe, ge) in enumerate(((x_v[e], g_v[e]), (xs[0, i], xs[1, i]))):
+            down_part = dot(a, xe, NN)
+            up_part = dot(b, ge, NN)
+            for h, part in ((ha, down_part), (hb, up_part)):
+                high, low = split(part[:k1] + part[k1:])
+                h[s, 0, at, :] = high
+                h[s, 1, at, :] = low
+        return carry
+
+    def combine(k):
         size = piece_e * k1
-        at = pl.ds(pl.multiple_of((h * half_e + k * piece_e) * k1, k1), size)
-        total = dot(ha[0, at, :], ra[...], NN) + dot(hb[0, at, :], rb[...], NN)
-        total = total + (dot(ha[1, at, :], ra[...], NN) + dot(hb[1, at, :], rb[...], NN))
-        total = total * scale
+        at = pl.ds(k * size, size)
+        total = 0.0
+        for s in range(2):
+            for h, r in ((ha, ra), (hb, rb)):
+                total = total + dot(jnp.concatenate([h[s, 0, at, :], h[s, 1, at, :]], axis=0), r[s], NN)
+        total = (total[:size] + total[size:]) * scale
         t[0, at, :] = total[:, :128]
         t[1, at, :] = total[:, 128:]
 
-    def arrive(k):
-        for i in reversed(range(len(chips))):
-            landed(k, i).wait_recv()
-            pass_on(k, chip_at(chips[i], -1)).start()
-
-    def project_piece(h, k):
-        lax.fori_loop(0, piece_e, project(h * half_e + k * piece_e), 0)
-        combine(h, k)
-
-    arrive(0)
-    project_piece(c, 0)
-    ring_on()
-    for k in range(1, np_):
-        arrive(k)
-        passed(k - 1).wait_recv()
-        project_piece(other, k - 1)
-        project_piece(c, k)
-    passed(np_ - 1).wait_recv()
-    project_piece(other, np_ - 1)
+    for k in range(np_):
+        landed(k).wait_recv()
+        for i in range(piece_e):
+            project(k * piece_e + i, 0)
+        combine(k)
     for a in range(k1):
-        cc, qq, al = (a // 2) % 2, a // 4, a % 2
         for side in range(2):
-            ts[cc, qq, al * el : (al + 1) * el, side * 128 : (side + 1) * 128] = t[
-                side, pl.ds(a, el, stride=k1), :
-            ]
-
-    swap = remote(ts.at[other], r3, s5.at[0], d5.at[0], sibling)
-    swap.start()
-    swap.wait_recv()
+            at = side * 2 * half_e + (a % 2) * half_e
+            ts[a // 2, at : at + half_e, :] = t[side, pl.ds(a, half_e, stride=k1), :]
 
     def scatter(i):
-        p = chip_at(chips[i])
-        return remote(ts.at[c, p], r4.at[i], s6.at[0], d6.at[0], chip(p))
-
-    scatter_all = remote(r4, r4, s6.at[0], d6.at[0], chip(q))
-
-    for i, shift in enumerate(chips):
-        p = chip_at(shift)
-        ts[c, p] += r3[p]
+        p = member(group[i])
+        return remote(ts.at[p], r4.at[i], s6.at[0], d6.at[0], (dp, p))
+
+    scatter_all = remote(r4, r4, s6.at[0], d6.at[0], (dp, m))
+
+    for i in range(len(group)):
         scatter(i).start()
-    total = ts[c, q] + r3[q]
 
     for hop in first_hop[2:] + second_hop:
         arrival(*hop).wait_recv()
@@ -374,9 +362,14 @@
     sc[...] = jnp.zeros_like(sc)
 
     scatter_all.wait_recv()
-    for j in range(1, nq):
-        total = total + r4[j - 1]
-    tg[yh] = total
+    mine, theirs = ts[m], 0.0
+    for i, shift in enumerate(group):
+        if shift[2]:
+            theirs = theirs + r4[i]
+        else:
+            mine = mine + r4[i]
+    tg[yh, 0:te] = jnp.where(c == 0, mine, theirs)
+    tg[yh, te : 2 * te] = jnp.where(c == 0, theirs, mine)
 
     def share(j):
         part = tg.at[yh]
@@ -387,20 +380,27 @@
         pl.semaphore_wait(near, len(sides))
     for j in lines:
         share(j).start()
-    tp_ref[:, 0:256] = total[0:el]
-    tp_ref[:, 256:512] = total[el:te]
+
+    def unfold(target, first, y):
+        for h in range(2):
+            for side in range(2):
+                for al in range(2):
+                    at = h * te + side * el + al * half_e
+                    lanes = al * 256 + side * 128
+                    target[first + h * half_e : first + (h + 1) * half_e, lanes : lanes + 128] = tg[y, at : at + half_e, :]
+
+    unfold(tp_ref, 0, yh)
     if nyh > 1:
         shared.wait_recv()
 
     for y in range(nyh):
-        for al in range(2):
-            lt[y * el : (y + 1) * el, al * 256 : (al + 1) * 256] = tg[y, al * el : (al + 1) * el, :]
+        unfold(lt, y * el, y)
     train = lt[...]
-    high, low = split(train)
-    scores = dot(high, vb[...], NT) + dot(low, vb[...], NT)
+    rows = nyh * el
+    scores = dot(jnp.concatenate(split(train), axis=0), vb[...], NT)
+    scores = scores[:rows] + scores[rows:]
     high, low = split(train * train)
     squares = (dot(ones, high, NT) + dot(ones, low, NT))[0:1]
-    rows = nyh * el
     for i in range(nmp):
         sc[i, 0:er, :] = scores[i * er : (i + 1) * er, 0:hv]
         sc[i, er : 2 * er, :] = scores[i * er : (i + 1) * er, hv : 2 * hv]
@@ -435,28 +435,28 @@
     row_o = lax.broadcasted_iota(jnp.int32, (8, 128), 0)
     lane_o = lax.broadcasted_iota(jnp.int32, (8, 128), 1)
     placed = jnp.full((8, 128), LOWEST, F32)
+    start = lax.rem(m, 4) * (er * nz)
     first_half = row_o < er
     e_of = jnp.where(first_half, row_o, row_o - er)
     for g in range(nz // 2):
         here = (lane_id >= g * vl) & (lane_id < (g + 1) * vl)
         best = jnp.max(jnp.where(here, cosines, LOWEST), axis=1, keepdims=True) * weight
-        lane = e_of * nz + jnp.where(first_half, 0, nz // 2) + g
+        lane = start + e_of * nz + jnp.where(first_half, 0, nz // 2) + g
         placed = jnp.where((lane_o == lane) & (row_o < 2 * er), best, placed)
-    mine = yh * nmp + m
-    fp[mine] = jnp.max(placed, axis=0, keepdims=True)
+    place = yh * nmp + m
+    fp[place] = jnp.max(placed, axis=0, keepdims=True)
 
     def tell(shift):
-        part = fp.at[mine]
+        part = fp.at[place]
         return remote(part, part, s9.at[0], d9.at[0], row(*neighbour(*shift)))
 
     told = remote(fp.at[pl.ds(0, len(others))], fp.at[pl.ds(0, len(others))], s9.at[0], d9.at[0], row(yh, m))
     for shift in others:
         tell(shift).start()
     told.wait_recv()
-    best = fp[0:nmp]
-    for y in range(1, nyh):
-        best = jnp.maximum(best, fp[y * nmp : (y + 1) * nmp])
-    fz[z] = best
+    best = [fp[4 * i : 4 * i + 4] for i in range(nyh * nmp // 4)]
+    for i in range(nmp // 4):
+        fz[z, i] = jnp.max(functools.reduce(jnp.maximum, best[i :: nmp // 4]), axis=0)
 
     def publish(j):
         part = fz.at[z]
@@ -469,10 +469,9 @@
     for k in range(np_):
         lend(k).wait_send()
         spread_all(k).wait_send()
-        passed(k).wait_send()
-        for i in range(len(chips)):
-            hand_out(k, i).wait_send()
-    swap.wait_send()
+        landed(k).wait_send()
+        for side in range(2):
+            trade(k, side).wait_send()
     scatter_all.wait_send()
     for hop in first_hop + second_hop:
         along(*hop).wait_send()
@@ -511,16 +510,18 @@
         pltpu.VMEM((2 * half_rows, tokens), F32),
         pltpu.VMEM((np_, piece_rows, tokens), F32),
         pltpu.VMEM((np_, nq - 1, chunk, tokens), F32),
-        pltpu.VMEM((2 * half_rows, tokens), F32),
-        pltpu.VMEM((width, k2), BF16),
-        pltpu.VMEM((width, k2), BF16),
-        pltpu.VMEM((2, el * k1, width), BF16),
-        pltpu.VMEM((2, el * k1, width), BF16),
-        pltpu.VMEM((2, el * k1, 128), F32),
-        pltpu.VMEM((2, nq, 2 * el, k2), F32),
-        pltpu.VMEM((nq, 2 * el, k2), F32),
-        pltpu.VMEM((nq - 1, 2 * el, k2), F32),
-        pltpu.VMEM((nyh, 2 * el, k2), F32),
+        pltpu.VMEM((half_rows, tokens), F32),
+        pltpu.VMEM((2, width, k2), BF16),
+        pltpu.VMEM((2, width, k2), BF16),
+        pltpu.VMEM((2, 2, el * k1 // 2, width), BF16),
+        pltpu.VMEM((2, 2, el * k1 // 2, width), BF16),
+        pltpu.VMEM((2, el * k1 // 2, 128), F32),
+        pltpu.VMEM((nmp, 2 * el, 128), F32),
+        pltpu.VMEM((nmp - 1, 2 * el, 128), F32),
+        pltpu.VMEM((2, el // 2, tokens, width), F32),
+        pltpu.VMEM((2, el // 2, tokens, width), F32),
+        pltpu.VMEM((2, el // 2, tokens, width), BF16),
+        pltpu.VMEM((nyh, 4 * el, 128), F32),
         pltpu.VMEM((nyh * el, kl), F32),
         pltpu.VMEM((nz, vl, kl), F32),
         pltpu.VMEM((nz * vl, kl), BF16),
@@ -529,7 +530,7 @@
         pltpu.VMEM((nmp, 8, hv), F32),
         pltpu.VMEM((nmp - 1, 8, hv), F32),
         pltpu.VMEM((nyh * nmp, 1, 128), F32),
-        pltpu.VMEM((nz, nmp, 1, 128), F32),
+        pltpu.VMEM((nz, nmp // 4, 1, 128), F32),
         dma((2, 2 * np_)),
         dma((6,)),
     ]
@@ -537,9 +538,8 @@
     for count in (
         (np_,),
         (np_,),
-        (np_, nq - 1),
         (np_,),
-        one,
+        (np_, 2),
         one,
         one,
         (nz,),
@@ -554,7 +554,7 @@
         functools.partial(kernel, nz, nyh, nq, np_, scale, root_k),
         out_shape=(
             jax.ShapeDtypeStruct((el, kl), F32),
-            jax.ShapeDtypeStruct((nz, nmp, 1, 128), F32),
+            jax.ShapeDtypeStruct((nz, nmp // 4, 1, 128), F32),
         ),
         in_specs=[pl.BlockSpec(memory_space=pltpu.HBM)] * len(args),
         out_specs=[pl.BlockSpec(memory_space=pltpu.VMEM)] * 2,
@@ -564,7 +564,7 @@
         ),
     )(*[pltpu.with_memory_space_constraint(a, pltpu.HBM) for a in args])
     er = nyh * el // nmp
-    influence = best.reshape(nz * nmp, 128)[:, : er * nz].reshape(nz * nmp * er, nz)
+    influence = best.reshape(nz * nmp // 4, 128)[:, : 4 * er * nz].reshape(nz * nmp * er, nz)
     return (train_proj, influence)
 
 

time: 57.1 us -> 53.7 us (0.940)
  Pallas kernels: 54.9 us -> 51.5 us
    pallas_call x1, Pallas kernels: 54.9 us -> 51.5 us  [on_device(): pl.pallas_call(functools.partial(kernel, nz, nyh, nq, np_, scale, root_k)...]
where the time goes in v4:
time: 53.7 us; the launch traced here: 53.6 us
  Pallas kernels  51.5 us (96%)
  local copies, waits for them, and re-layouts  1.43 us (3%)
  between operations  0.65 us (1%)
    pallas_call x1, Pallas kernels, on_device(): pl.pallas_call(functools.partial(kernel, nz, nyh, nq, np_, scale, root_k)...  51.5 us
    unnamed x2, local copies, waits for them, and re-layouts  1.32 us

profile of v4, /device:TPU:1, one launch (start us, length us, event | category | flops | bytes accessed | tf_op | source)
XLA Modules:
  0.0 53.6 jit_solution(18128694623390166728)
XLA Ops:
  0.6 51.5 %shard_map.95 = (f32[12,512]{1,0:T(8,128)S(1)}, f32[8,4,1,128]{3,2,1,0:T(1,128)S(1)}) custom-call(bf16[12,256,256]{2,1,0:T(8,128)(2,1)} %refs_0_.1, bf16[12,256,256]{2,1,0:T(8,128)(2,1)} %refs_1_.1, s32[12]{0:T(128)} %refs_2_.1, bf16[128,256]{1,0:T(8,128)(2,1)} %refs_3_.1, bf16[256,128]{1,0:T(8,128)(2,1)} %refs_4_.1, s32[2,256]{1,0:T(2,128)} %refs_5_.1, ...), custom_call_target="tpu_custom_call" | custom-call | tf_op jit(solution)/shard_map/pallas_call | solution.py:553
  52.2 0.1 reshape.11
  52.3 0.7 %copy.10 = f32[384,8]{0,1:T(8,128)} copy(f32[384,8]{1,0:T(8,128)S(1)} %reshape.11) | data formatting | bytes 24576
  53.0 0.6 %copy.12 = f32[12,512]{1,0:T(8,128)} copy(f32[12,512]{1,0:T(8,128)S(1)} %get-tuple-element.10) | data formatting | bytes 49152

commit v5 on v4

--- a/solution.py
+++ b/solution.py
@@ -42,9 +42,9 @@
     (
         (x_ref, g_ref, len_ref, red_ref, exp_ref, wseed_ref, rseed_ref, val_ref, tp_ref, inf_ref),
         (x_v, g_v, len_v, red_v, exp_v, wseed_v, rseed_v, rpad, val_v, u, r1, r2, uf, ra, rb, ha, hb, t, ts, r4, xf, xr, xs),
-        (tg, lt, vf, vb, vq, rq, sc, r5, fp, fz),
-        (in_sem, small_sem, s1, d1, s2, d2, s3, d3, s4, d4, s6, d6, s7, d7, sv, dv, sq, dq, s8, d8, s9, d9, s10, d10, near),
-    ) = refs[:10], refs[10:33], refs[33:43], refs[43:]
+        (tg, tm, tx, lt, vf, vb, vq, rq, sc, r5, fp, fz),
+        (in_sem, small_sem, s1, d1, s2, d2, s3, d3, s4, d4, s6, d6, s7, d7, sv, dv, sq, dq, s8, d8, s9, d9, s10, d10, near, near2, far),
+    ) = refs[:10], refs[10:33], refs[33:45], refs[45:]
     nmp = 2 * nq
     el = x_v.shape[0]
     k1 = nmp * 2
@@ -81,7 +81,7 @@
     chips.sort(key=lambda d: -(d[0] + ring_hops(d[1], nx)))
     group = [(dy, dx, dc) for dy in range(2) for dx in range(nx) for dc in range(2) if (dy, dx, dc) != (0, 0, 0)]
     group.sort(key=lambda d: -(d[0] + ring_hops(d[1], nx)))
-    planes = sorted(range(1, nz), key=lambda d: -ring_hops(d, nz))
+    depths = sorted(range(1, nz), key=lambda d: -ring_hops(d, nz))
     lines = sorted(range(1, nyh), key=lambda d: -ring_hops(d, nyh))
 
     def chip_at(shift, sign=1):
@@ -107,7 +107,7 @@
     pieces = [(h, k) for h in (other, c) for k in range(np_)]
 
     def examples(h, k):
-        return pl.ds(h * half_e + k * piece_e, piece_e)
+        return pl.ds((2 * k + h) * piece_e, piece_e)
 
     inputs = []
     for i, (h, k) in enumerate(pieces):
@@ -134,14 +134,22 @@
         copy.start()
 
     barrier = pltpu.get_barrier_semaphore()
-    shifts = (2, -2, 1, -1) if nz == 8 else (1, -1)
-    sides = [j for j in (1, nyh - 1) if j < nyh][: nyh - 1]
-    sides = sides[:1] if nyh == 2 else sides
-    near_by = [sibling] + [chip(chip_at(shift)) for shift in chips]
-    near_by += [column(lax.rem(z + nz + d, nz)) for d in shifts]
-    near_by += [row(lax.rem(yh + j, nyh), m) for j in sides]
-    for device in near_by:
-        pl.semaphore_signal(barrier, inc=1, device_id=device, device_id_type=MESH)
+
+    def turns(n):
+        return sorted({1 % n, (n - 1) % n} - {0})
+
+    def along_y(s):
+        y = lax.rem(2 * yh + ylo + s, 2 * nyh)
+        return (z * nyh + lax.div(y, 2), 2 * (lax.rem(y, 2) * nx + x) + c)
+
+    def signal(semaphore, device):
+        pl.semaphore_signal(semaphore, inc=1, device_id=device, device_id_type=MESH)
+
+    in_plane = [chip(chip_at((0, s))) for s in turns(nx)] + [along_y(s) for s in turns(2 * nyh)]
+    planes = [column(lax.rem(z + s, nz)) for s in turns(nz)]
+    sides = turns(nyh)
+    for device in [sibling] + in_plane + planes:
+        signal(barrier, device)
     for copy in [small[3]] + [copy for pair in inputs[1:] for copy in pair] + small[4:]:
         copy.start()
 
@@ -165,13 +173,13 @@
 
     lane_t = lax.broadcasted_iota(jnp.int32, (k1, tokens), 1)
 
-    def sketch(first):
+    def sketch(h, k):
         def body(i, carry):
-            e = first + i
+            e = (2 * k + h) * piece_e + i
             kept = lane_t < len_v[e]
             out = dot(p_out, g_v[e], NT)
             inn = dot(p_in, x_v[e], NT)
-            base = pl.multiple_of(e * per, per)
+            base = pl.multiple_of(h * half_rows + k * piece_rows + i * per, per)
             u[pl.ds(base, k1), :] = jnp.where(kept, out[:k1] + out[k1:], 0.0)
             u[pl.ds(base + k1, k1), :] = jnp.where(kept, inn[:k1] + inn[k1:], 0.0)
             return carry
@@ -182,7 +190,7 @@
         h, k = pieces[i]
         for copy in inputs[i]:
             copy.wait()
-        lax.fori_loop(0, piece_e, sketch(h * half_e + k * piece_e), 0, unroll=True)
+        lax.fori_loop(0, piece_e, sketch(h, k), 0, unroll=True)
 
     def rows_of(h, k):
         return pl.ds(pl.multiple_of(h * half_rows + k * piece_rows, piece_rows), piece_rows)
@@ -202,13 +210,16 @@
 
     def borrowed(k, p):
         return u[chunk_of(c, k, p), :] + r1[k, pl.ds(pl.multiple_of(p * chunk, chunk), chunk), :]
+
+    outer = [i for i, shift in enumerate(chips) if shift[0] + ring_hops(shift[1], nx) > 2]
 
     def spread_piece(k):
         lend(k).wait_recv()
         for i, shift in enumerate(chips):
             p = chip_at(shift)
             u[chunk_of(c, k, p), :] = borrowed(k, p)
-            spread(k, i).start()
+            if k or i not in outer:
+                spread(k, i).start()
 
     def along(i, offset, shift, part):
         at = lax.rem(z + nz + offset, nz)
@@ -220,26 +231,37 @@
         block = vf.at[at] if part is None else vf.at[at, pl.ds(part * (vl // 2), vl // 2)]
         return remote(block, block, sv.at[i], dv.at[i], column(lax.rem(z + nz - shift, nz)))
 
-    first_hop = [(i, 0, d, None) for i, d in enumerate(shifts)]
+    first_hop = [(0, 0, 1, None), (1, 0, -1, None)]
     if nz == 8:
-        second_hop = [(4, -2, 1, None), (5, 2, -1, None), (6, -2, 2, 0), (7, 2, -2, 1)]
+        second_hop = [(2, -1, 1, None), (3, 1, -1, None)]
+        third_hop = [(4, -2, 1, None), (5, 2, -1, None), (6, -2, 2, 0), (7, 2, -2, 1)]
     else:
-        second_hop = [(2, -1, 1, 0), (3, 1, -1, 1)]
-
-    for k in range(np_ + 1):
-        sketch_piece(k)
-    pl.semaphore_wait(barrier, len(near_by))
-    for k in range(np_):
-        lend(k).start()
-    for j in sides:
-        pl.semaphore_signal(near, inc=1, device_id=row(lax.rem(yh + j, nyh), m), device_id_type=MESH)
+        second_hop = []
+        third_hop = [(2, -1, 1, 0), (3, 1, -1, 1)]
+
+    sketch_piece(0)
+    pl.semaphore_wait(barrier, 1 + len(in_plane) + len(planes))
+    lend(0).start()
+    for device in in_plane:
+        signal(near, device)
     small[4].wait()
     vf[z] = val_v[...].astype(F32)
     for hop in first_hop:
         along(*hop).start()
-    for k in range(np_):
-        if k:
-            sketch_piece(np_ + k)
+    for k in range(1, np_):
+        sketch_piece(k)
+        lend(k).start()
+    sketch_piece(np_)
+    pl.semaphore_wait(near, len(in_plane))
+    signal(near2, (dp, 2 * chip_at((1, 0)) + c))
+    for j in sides:
+        signal(far, row(lax.rem(yh + j, nyh), m))
+    spread_piece(0)
+    pl.semaphore_wait(near2, 1)
+    for i in outer:
+        spread(0, i).start()
+    for k in range(1, np_):
+        sketch_piece(np_ + k)
         spread_piece(k)
 
     def trade(k, side):
@@ -250,7 +272,7 @@
         for side, tokens_v in enumerate((x_v, g_v)):
 
             def widen(i, carry, side=side, tokens_v=tokens_v, k=k):
-                xf[side, k * piece_e + i] = tokens_v[other * half_e + k * piece_e + i].astype(F32)
+                xf[side, k * piece_e + i] = tokens_v[(2 * k + other) * piece_e + i].astype(F32)
                 return carry
 
             lax.fori_loop(0, piece_e, widen, 0)
@@ -261,6 +283,10 @@
         columns = device * width + lax.broadcasted_iota(jnp.int32, (width, wseed_v.shape[1]), 0)
         ra[s] = sign_of(wseed_v[0:1, :], columns).astype(BF16)
         rb[s] = sign_of(wseed_v[1:2, :], columns).astype(BF16)
+    for hop in first_hop:
+        arrival(*hop).wait_recv()
+    for hop in second_hop:
+        along(*hop).start()
 
     def hand_out(k, i):
         part = uf.at[chunk_of(0, k, q)]
@@ -278,12 +304,6 @@
         for i in range(len(chips)):
             hand_out(k, i).start()
 
-    def ring_on():
-        for hop in first_hop[:2]:
-            arrival(*hop).wait_recv()
-        for hop in second_hop:
-            along(*hop).start()
-
     for k in range(np_):
         for side in range(2):
             trade(k, side).wait_recv()
@@ -293,14 +313,18 @@
                 return carry
 
             lax.fori_loop(0, piece_e, narrow_tokens, 0)
-    ring_on()
-
-    def project(i, carry):
+    for hop in second_hop[:2]:
+        arrival(*hop).wait_recv()
+    for hop in third_hop:
+        along(*hop).start()
+
+    def project(k, j):
+        i = k * piece_e + j
         base = i * per
         a = jnp.concatenate(split(uf[pl.ds(base, k1), :]), axis=0)
         b = jnp.concatenate(split(uf[pl.ds(base + k1, k1), :]), axis=0)
         at = pl.ds(i * k1, k1)
-        e = c * half_e + i
+        e = (2 * k + c) * piece_e + j
         for s, (xe, ge) in enumerate(((x_v[e], g_v[e]), (xs[0, i], xs[1, i]))):
             down_part = dot(a, xe, NN)
             up_part = dot(b, ge, NN)
@@ -308,7 +332,6 @@
                 high, low = split(part[:k1] + part[k1:])
                 h[s, 0, at, :] = high
                 h[s, 1, at, :] = low
-        return carry
 
     def combine(k):
         size = piece_e * k1
@@ -321,26 +344,71 @@
         t[0, at, :] = total[:, :128]
         t[1, at, :] = total[:, 128:]
 
+    block = 4 * piece_e
+
+    def block_of(p):
+        return pl.ds(pl.multiple_of(p * block, block), block)
+
+    def regroup(k):
+        for side in range(2):
+            for al in range(2):
+                for j in range(piece_e):
+                    to = pl.ds((2 * side + al) * piece_e + j, nmp, stride=block)
+                    ts[k, to, :] = t[side, pl.ds((k * piece_e + j) * k1 + al, nmp, stride=2), :]
+
+    def scatter(k, i):
+        p = member(group[i])
+        return remote(ts.at[k, block_of(p)], r4.at[k, i], s6.at[k], d6.at[k], (dp, p))
+
+    def scatter_all(k):
+        return remote(r4.at[k], r4.at[k], s6.at[k], d6.at[k], (dp, m))
+
     for k in range(np_):
         landed(k).wait_recv()
-        for i in range(piece_e):
-            project(k * piece_e + i, 0)
+        for j in range(piece_e):
+            project(k, j)
         combine(k)
-    for a in range(k1):
+        regroup(k)
+        for i in range(len(group)):
+            scatter(k, i).start()
+
+    each = 2 * block
+
+    def share(k, j):
+        part = tg.at[pl.ds(pl.multiple_of((yh * np_ + k) * each, each), each)]
+        return remote(part, part, s7.at[k], d7.at[k], row(lax.rem(yh + j, nyh), m))
+
+    def shared(k):
+        part = tg.at[pl.ds(0, (nyh - 1) * each)]
+        return remote(part, part, s7.at[k], d7.at[k], row(yh, m))
+
+    if sides:
+        pl.semaphore_wait(far, len(sides))
+    for k in range(np_):
+        scatter_all(k).wait_recv()
+        mine, theirs = ts[k, block_of(m), :], 0.0
+        for i, shift in enumerate(group):
+            if shift[2]:
+                theirs = theirs + r4[k, i]
+            else:
+                mine = mine + r4[k, i]
+        pair = jnp.concatenate([jnp.where(c == 0, mine, theirs), jnp.where(c == 0, theirs, mine)], axis=0)
+        tg[pl.ds(pl.multiple_of((yh * np_ + k) * each, each), each), :] = pair
+        tm[k * each : (k + 1) * each, :] = pair
+        for j in lines:
+            share(k, j).start()
+
+    def unfold(target, source, first, at):
         for side in range(2):
-            at = side * 2 * half_e + (a % 2) * half_e
-            ts[a // 2, at : at + half_e, :] = t[side, pl.ds(a, half_e, stride=k1), :]
-
-    def scatter(i):
-        p = member(group[i])
-        return remote(ts.at[p], r4.at[i], s6.at[0], d6.at[0], (dp, p))
-
-    scatter_all = remote(r4, r4, s6.at[0], d6.at[0], (dp, m))
-
-    for i in range(len(group)):
-        scatter(i).start()
-
-    for hop in first_hop[2:] + second_hop:
+            for al in range(2):
+                for j in range(piece_e):
+                    rows = pl.ds(at + (2 * side + al) * piece_e + j, 2 * np_, stride=block)
+                    target[2 * al + side, pl.ds(first + j, 2 * np_, stride=piece_e), :] = source[rows, :]
+
+    unfold(tx, tm, 0, 0)
+    for i in range(4):
+        tp_ref[:, i * 128 : (i + 1) * 128] = tx[i]
+    for hop in second_hop[2:] + third_hop:
         arrival(*hop).wait_recv()
 
     def narrow(i, carry):
@@ -361,41 +429,13 @@
         tally(i).start()
     sc[...] = jnp.zeros_like(sc)
 
-    scatter_all.wait_recv()
-    mine, theirs = ts[m], 0.0
-    for i, shift in enumerate(group):
-        if shift[2]:
-            theirs = theirs + r4[i]
-        else:
-            mine = mine + r4[i]
-    tg[yh, 0:te] = jnp.where(c == 0, mine, theirs)
-    tg[yh, te : 2 * te] = jnp.where(c == 0, theirs, mine)
-
-    def share(j):
-        part = tg.at[yh]
-        return remote(part, part, s7.at[0], d7.at[0], row(lax.rem(yh + j, nyh), m))
-
-    shared = remote(tg.at[pl.ds(0, nyh - 1)], tg.at[pl.ds(0, nyh - 1)], s7.at[0], d7.at[0], row(yh, m))
-    if sides:
-        pl.semaphore_wait(near, len(sides))
-    for j in lines:
-        share(j).start()
-
-    def unfold(target, first, y):
-        for h in range(2):
-            for side in range(2):
-                for al in range(2):
-                    at = h * te + side * el + al * half_e
-                    lanes = al * 256 + side * 128
-                    target[first + h * half_e : first + (h + 1) * half_e, lanes : lanes + 128] = tg[y, at : at + half_e, :]
-
-    unfold(tp_ref, 0, yh)
     if nyh > 1:
-        shared.wait_recv()
+        for k in range(np_):
+            shared(k).wait_recv()
 
     for y in range(nyh):
-        unfold(lt, y * el, y)
-    train = lt[...]
+        unfold(lt, tg, y * el, y * np_ * each)
+    train = jnp.concatenate([lt[i] for i in range(4)], axis=1)
     rows = nyh * el
     scores = dot(jnp.concatenate(split(train), axis=0), vb[...], NT)
     scores = scores[:rows] + scores[rows:]
@@ -463,7 +503,7 @@
         return remote(part, part, s10.at[0], d10.at[0], column(lax.rem(z + j, nz)))
 
     published = remote(fz.at[pl.ds(0, nz - 1)], fz.at[pl.ds(0, nz - 1)], s10.at[0], d10.at[0], column(z))
-    for j in planes:
+    for j in depths:
         publish(j).start()
 
     for k in range(np_):
@@ -472,12 +512,14 @@
         landed(k).wait_send()
         for side in range(2):
             trade(k, side).wait_send()
-    scatter_all.wait_send()
-    for hop in first_hop + second_hop:
+    for k in range(np_):
+        scatter_all(k).wait_send()
+    for hop in first_hop + second_hop + third_hop:
         along(*hop).wait_send()
     tally_all.wait_send()
     if nyh > 1:
-        shared.wait_send()
+        for k in range(np_):
+            shared(k).wait_send()
     deal_all.wait_send()
     told.wait_send()
     published.wait_recv()
@@ -516,13 +558,15 @@
         pltpu.VMEM((2, 2, el * k1 // 2, width), BF16),
         pltpu.VMEM((2, 2, el * k1 // 2, width), BF16),
         pltpu.VMEM((2, el * k1 // 2, 128), F32),
-        pltpu.VMEM((nmp, 2 * el, 128), F32),
-        pltpu.VMEM((nmp - 1, 2 * el, 128), F32),
+        pltpu.VMEM((np_, nmp * 2 * el // np_, 128), F32),
+        pltpu.VMEM((np_, nmp - 1, 2 * el // np_, 128), F32),
         pltpu.VMEM((2, el // 2, tokens, width), F32),
         pltpu.VMEM((2, el // 2, tokens, width), F32),
         pltpu.VMEM((2, el // 2, tokens, width), BF16),
-        pltpu.VMEM((nyh, 4 * el, 128), F32),
-        pltpu.VMEM((nyh * el, kl), F32),
+        pltpu.VMEM((nyh * 4 * el, 128), F32),
+        pltpu.VMEM((4 * el, 128), F32),
+        pltpu.VMEM((4, el, 128), F32),
+        pltpu.VMEM((4, nyh * el, 128), F32),
         pltpu.VMEM((nz, vl, kl), F32),
         pltpu.VMEM((nz * vl, kl), BF16),
         pltpu.VMEM((1, 1, nz * vl), F32),
@@ -540,8 +584,8 @@
         (np_,),
         (np_,),
         (np_, 2),
-        one,
-        one,
+        (np_,),
+        (np_,),
         (nz,),
         one,
         one,
@@ -549,7 +593,7 @@
         one,
     ):
         scratch += [dma(count), dma(count)]
-    scratch.append(pltpu.SemaphoreType.REGULAR)
+    scratch += [pltpu.SemaphoreType.REGULAR] * 3
     train_proj, best = pl.pallas_call(
         functools.partial(kernel, nz, nyh, nq, np_, scale, root_k),
         out_shape=(
@@ -568,7 +612,7 @@
     return (train_proj, influence)
 
 
-def solution(mesh, nyh=4, np_=2):
+def solution(mesh, nyh=4, np_=3):
     ndp, nmp = mesh.shape["dp"], mesh.shape["mp"]
     nz, nq = ndp // nyh, nmp // 2
     width = nmp * 256

time: 53.7 us -> 52.1 us (0.970)
  Pallas kernels: 51.5 us -> 49.9 us
    pallas_call x1, Pallas kernels: 51.5 us -> 49.9 us  [on_device(): pl.pallas_call(functools.partial(kernel, nz, nyh, nq, np_, scale, root_k)...]
where the time goes in v5:
time: 52.1 us; the launch traced here: 52 us
  Pallas kernels  49.9 us (96%)
  local copies, waits for them, and re-layouts  1.43 us (3%)
  between operations  0.65 us (1%)
    pallas_call x1, Pallas kernels, on_device(): pl.pallas_call(functools.partial(kernel, nz, nyh, nq, np_, scale, root_k)...  49.9 us
    unnamed x2, local copies, waits for them, and re-layouts  1.32 us

profile of v5, /device:TPU:1, one launch (start us, length us, event | category | flops | bytes accessed | tf_op | source)
XLA Modules:
  0.0 52.0 jit_solution(1169232961796166457)
XLA Ops:
  0.6 49.9 %shard_map.95 = (f32[12,512]{1,0:T(8,128)S(1)}, f32[8,4,1,128]{3,2,1,0:T(1,128)S(1)}) custom-call(bf16[12,256,256]{2,1,0:T(8,128)(2,1)} %refs_0_.1, bf16[12,256,256]{2,1,0:T(8,128)(2,1)} %refs_1_.1, s32[12]{0:T(128)} %refs_2_.1, bf16[128,256]{1,0:T(8,128)(2,1)} %refs_3_.1, bf16[256,128]{1,0:T(8,128)(2,1)} %refs_4_.1, s32[2,256]{1,0:T(2,128)} %refs_5_.1, ...), custom_call_target="tpu_custom_call" | custom-call | tf_op jit(solution)/shard_map/pallas_call | solution.py:597
  50.6 0.1 reshape.11
  50.7 0.7 %copy.10 = f32[384,8]{0,1:T(8,128)} copy(f32[384,8]{1,0:T(8,128)S(1)} %reshape.11) | data formatting | bytes 24576
  51.4 0.6 %copy.12 = f32[12,512]{1,0:T(8,128)} copy(f32[12,512]{1,0:T(8,128)S(1)} %get-tuple-element.10) | data formatting | bytes 49152

commit v6 on v5

--- a/solution.py
+++ b/solution.py
@@ -106,31 +106,33 @@
 
     pieces = [(h, k) for h in (other, c) for k in range(np_)]
 
-    def examples(h, k):
-        return pl.ds((2 * k + h) * piece_e, piece_e)
-
-    inputs = []
-    for i, (h, k) in enumerate(pieces):
-        inputs.append(
-            (
-                pltpu.make_async_copy(x_ref.at[examples(h, k)], x_v.at[examples(h, k)], in_sem.at[0, i]),
-                pltpu.make_async_copy(g_ref.at[examples(h, k)], g_v.at[examples(h, k)], in_sem.at[1, i]),
-            )
-        )
+    def examples(k):
+        return pl.ds(2 * k * piece_e, 2 * piece_e)
+
+    inputs = [
+        [
+            pltpu.make_async_copy(a.at[examples(k)], b.at[examples(k)], in_sem.at[k])
+            for a, b in ((x_ref, x_v), (g_ref, g_v))
+        ]
+        for k in range(np_)
+    ]
+
+    def inputs_in(k):
+        both = pl.ds(0, 4 * piece_e)
+        pltpu.make_async_copy(x_ref.at[both], x_v.at[both], in_sem.at[k]).wait()
+
     small = [
         pltpu.make_async_copy(a, b, small_sem.at[i])
-        for i, (a, b) in enumerate(
-            (
-                (rseed_ref, rseed_v),
-                (red_ref, red_v),
-                (exp_ref, exp_v),
-                (len_ref, len_v),
-                (val_ref, val_v),
-                (wseed_ref, wseed_v),
-            )
+        for i, a, b in (
+            (0, rseed_ref, rseed_v),
+            (1, red_ref, red_v),
+            (1, exp_ref, exp_v),
+            (2, len_ref, len_v),
+            (3, val_ref, val_v),
+            (4, wseed_ref, wseed_v),
         )
     ]
-    for copy in small[:3] + list(inputs[0]):
+    for copy in small[:4] + inputs[0]:
         copy.start()
 
     barrier = pltpu.get_barrier_semaphore()
@@ -150,7 +152,7 @@
     sides = turns(nyh)
     for device in [sibling] + in_plane + planes:
         signal(barrier, device)
-    for copy in [small[3]] + [copy for pair in inputs[1:] for copy in pair] + small[4:]:
+    for copy in small[4:5] + [copy for pair in inputs[1:] for copy in pair] + small[5:]:
         copy.start()
 
     others = [(dyh, *shift) for dyh in range(nyh) for shift in [(0, 0, 0)] + group if (dyh, *shift) != (0, 0, 0, 0)]
@@ -165,8 +167,7 @@
     ranks = lax.broadcasted_iota(jnp.int32, (128, 128), 0)
     left_a = sign_of(rpad[0:1, :], ranks).T[0:k1].astype(BF16)
     left_b = sign_of(rpad[1:2, :], ranks).T[0:k1].astype(BF16)
-    small[1].wait()
-    small[2].wait()
+    pltpu.make_async_copy(x_ref.at[0], x_v.at[0], small_sem.at[1]).wait()
     p_out = jnp.concatenate(split(dot(left_a, exp_v[...], NT)), axis=0)
     p_in = jnp.concatenate(split(dot(left_b, red_v[...], NN)), axis=0)
     small[3].wait()
@@ -188,8 +189,8 @@
 
     def sketch_piece(i):
         h, k = pieces[i]
-        for copy in inputs[i]:
-            copy.wait()
+        if i < np_:
+            inputs_in(k)
         lax.fori_loop(0, piece_e, sketch(h, k), 0, unroll=True)
 
     def rows_of(h, k):
@@ -199,14 +200,14 @@
         return pl.ds(pl.multiple_of(h * half_rows + k * piece_rows + p * chunk, chunk), chunk)
 
     def lend(k):
-        return remote(u.at[rows_of(other, k)], r1.at[k], s1.at[k], d1.at[k], sibling)
+        return remote(u.at[rows_of(other, k)], r1.at[k], s1.at[0], d1.at[k], sibling)
 
     def spread(k, i):
         p = chip_at(chips[i])
-        return remote(u.at[chunk_of(c, k, p)], r2.at[k, i], s2.at[k], d2.at[k], chip(p))
+        return remote(u.at[chunk_of(c, k, p)], r2.at[k, i], s2.at[0], d2.at[k], chip(p))
 
     def spread_all(k):
-        return remote(r2.at[k], r2.at[k], s2.at[k], d2.at[k], chip(q))
+        return remote(r2.at[k], r2.at[k], s2.at[0], d2.at[k], chip(q))
 
     def borrowed(k, p):
         return u[chunk_of(c, k, p), :] + r1[k, pl.ds(pl.multiple_of(p * chunk, chunk), chunk), :]
@@ -224,20 +225,19 @@
     def along(i, offset, shift, part):
         at = lax.rem(z + nz + offset, nz)
         block = vf.at[at] if part is None else vf.at[at, pl.ds(part * (vl // 2), vl // 2)]
-        return remote(block, block, sv.at[i], dv.at[i], column(lax.rem(z + nz + shift, nz)))
-
-    def arrival(i, offset, shift, part):
-        at = lax.rem(z + 2 * nz + offset - shift, nz)
-        block = vf.at[at] if part is None else vf.at[at, pl.ds(part * (vl // 2), vl // 2)]
-        return remote(block, block, sv.at[i], dv.at[i], column(lax.rem(z + nz - shift, nz)))
-
-    first_hop = [(0, 0, 1, None), (1, 0, -1, None)]
+        return remote(block, block, sv.at[0], dv.at[i], column(lax.rem(z + nz + shift, nz)))
+
+    def arrived(i, blocks):
+        block = vf.at[pl.ds(0, blocks)]
+        return remote(block, block, sv.at[0], dv.at[i], column(z))
+
+    first_hop = [(0, 0, 1, None), (0, 0, -1, None)]
     if nz == 8:
-        second_hop = [(2, -1, 1, None), (3, 1, -1, None)]
-        third_hop = [(4, -2, 1, None), (5, 2, -1, None), (6, -2, 2, 0), (7, 2, -2, 1)]
+        second_hop = [(1, -1, 1, None), (1, 1, -1, None)]
+        third_hop = [(2, -2, 1, None), (2, 2, -1, None), (2, -2, 2, 0), (2, 2, -2, 1)]
     else:
         second_hop = []
-        third_hop = [(2, -1, 1, 0), (3, 1, -1, 1)]
+        third_hop = [(2, -1, 1, 0), (2, 1, -1, 1)]
 
     sketch_piece(0)
     pl.semaphore_wait(barrier, 1 + len(in_plane) + len(planes))
@@ -257,16 +257,20 @@
     for j in sides:
         signal(far, row(lax.rem(yh + j, nyh), m))
     spread_piece(0)
+    ahead = min(1, np_ - 1)
+    for k in range(1, ahead + 1):
+        sketch_piece(np_ + k)
     pl.semaphore_wait(near2, 1)
     for i in outer:
         spread(0, i).start()
     for k in range(1, np_):
-        sketch_piece(np_ + k)
+        if k > ahead:
+            sketch_piece(np_ + k)
         spread_piece(k)
 
     def trade(k, side):
         part = pl.ds(k * piece_e, piece_e)
-        return remote(xf.at[side, part], xr.at[side, part], s4.at[k, side], d4.at[k, side], sibling)
+        return remote(xf.at[side, part], xr.at[side, part], s4.at[0], d4.at[k], sibling)
 
     for k in range(np_):
         for side, tokens_v in enumerate((x_v, g_v)):
@@ -283,17 +287,16 @@
         columns = device * width + lax.broadcasted_iota(jnp.int32, (width, wseed_v.shape[1]), 0)
         ra[s] = sign_of(wseed_v[0:1, :], columns).astype(BF16)
         rb[s] = sign_of(wseed_v[1:2, :], columns).astype(BF16)
-    for hop in first_hop:
-        arrival(*hop).wait_recv()
+    arrived(0, 2).wait_recv()
     for hop in second_hop:
         along(*hop).start()
 
     def hand_out(k, i):
         part = uf.at[chunk_of(0, k, q)]
-        return remote(part, part, s3.at[k], d3.at[k], chip(chip_at(chips[i])))
+        return remote(part, part, s3.at[0], d3.at[k], chip(chip_at(chips[i])))
 
     def landed(k):
-        return remote(r2.at[k], r2.at[k], s3.at[k], d3.at[k], chip(q))
+        return remote(r2.at[k], r2.at[k], s3.at[0], d3.at[k], chip(q))
 
     for k in range(np_):
         own = borrowed(k, q)
@@ -305,16 +308,17 @@
             hand_out(k, i).start()
 
     for k in range(np_):
+        traded = xr.at[0, pl.ds(0, 2 * piece_e)]
+        remote(traded, traded, s4.at[0], d4.at[k], sibling).wait_recv()
         for side in range(2):
-            trade(k, side).wait_recv()
 
             def narrow_tokens(i, carry, side=side, k=k):
                 xs[side, k * piece_e + i] = xr[side, k * piece_e + i].astype(BF16)
                 return carry
 
             lax.fori_loop(0, piece_e, narrow_tokens, 0)
-    for hop in second_hop[:2]:
-        arrival(*hop).wait_recv()
+    if second_hop:
+        arrived(1, 2).wait_recv()
     for hop in third_hop:
         along(*hop).start()
 
@@ -358,10 +362,10 @@
 
     def scatter(k, i):
         p = member(group[i])
-        return remote(ts.at[k, block_of(p)], r4.at[k, i], s6.at[k], d6.at[k], (dp, p))
+        return remote(ts.at[k, block_of(p)], r4.at[k, i], s6.at[0], d6.at[k], (dp, p))
 
     def scatter_all(k):
-        return remote(r4.at[k], r4.at[k], s6.at[k], d6.at[k], (dp, m))
+        return remote(r4.at[k], r4.at[k], s6.at[0], d6.at[k], (dp, m))
 
     for k in range(np_):
         landed(k).wait_recv()
@@ -376,11 +380,11 @@
 
     def share(k, j):
         part = tg.at[pl.ds(pl.multiple_of((yh * np_ + k) * each, each), each)]
-        return remote(part, part, s7.at[k], d7.at[k], row(lax.rem(yh + j, nyh), m))
+        return remote(part, part, s7.at[0], d7.at[k], row(lax.rem(yh + j, nyh), m))
 
     def shared(k):
         part = tg.at[pl.ds(0, (nyh - 1) * each)]
-        return remote(part, part, s7.at[k], d7.at[k], row(yh, m))
+        return remote(part, part, s7.at[0], d7.at[k], row(yh, m))
 
     if sides:
         pl.semaphore_wait(far, len(sides))
@@ -408,8 +412,7 @@
     unfold(tx, tm, 0, 0)
     for i in range(4):
         tp_ref[:, i * 128 : (i + 1) * 128] = tx[i]
-    for hop in second_hop[2:] + third_hop:
-        arrival(*hop).wait_recv()
+    arrived(2, nz - 5 if second_hop else nz - 3).wait_recv()
 
     def narrow(i, carry):
         vb[pl.ds(pl.multiple_of(i * vl, vl), vl), :] = vf[i].astype(BF16)
@@ -506,20 +509,16 @@
     for j in depths:
         publish(j).start()
 
-    for k in range(np_):
-        lend(k).wait_send()
-        spread_all(k).wait_send()
-        landed(k).wait_send()
-        for side in range(2):
-            trade(k, side).wait_send()
-    for k in range(np_):
-        scatter_all(k).wait_send()
-    for hop in first_hop + second_hop + third_hop:
-        along(*hop).wait_send()
+    remote(r1, r1, s1.at[0], d1.at[0], sibling).wait_send()
+    remote(r2, r2, s2.at[0], d2.at[0], sibling).wait_send()
+    remote(r2, r2, s3.at[0], d3.at[0], sibling).wait_send()
+    remote(xr, xr, s4.at[0], d4.at[0], sibling).wait_send()
+    remote(r4, r4, s6.at[0], d6.at[0], sibling).wait_send()
+    arrived(0, nz - 1).wait_send()
     tally_all.wait_send()
     if nyh > 1:
-        for k in range(np_):
-            shared(k).wait_send()
+        sent = tg.at[pl.ds(0, (nyh - 1) * np_ * each)]
+        remote(sent, sent, s7.at[0], d7.at[0], sibling).wait_send()
     deal_all.wait_send()
     told.wait_send()
     published.wait_recv()
@@ -575,24 +574,11 @@
         pltpu.VMEM((nmp - 1, 8, hv), F32),
         pltpu.VMEM((nyh * nmp, 1, 128), F32),
         pltpu.VMEM((nz, nmp // 4, 1, 128), F32),
-        dma((2, 2 * np_)),
-        dma((6,)),
+        dma((np_,)),
+        dma((5,)),
     ]
-    one = (1,)
-    for count in (
-        (np_,),
-        (np_,),
-        (np_,),
-        (np_, 2),
-        (np_,),
-        (np_,),
-        (nz,),
-        one,
-        one,
-        one,
-        one,
-    ):
-        scratch += [dma(count), dma(count)]
+    for receives in (np_,) * 6 + (3,) + (1,) * 4:
+        scratch += [dma((1,)), dma((receives,))]
     scratch += [pltpu.SemaphoreType.REGULAR] * 3
     train_proj, best = pl.pallas_call(
         functools.partial(kernel, nz, nyh, nq, np_, scale, root_k),

time: 52.1 us -> 51.4 us (0.987)
  Pallas kernels: 49.9 us -> 49.2 us
    pallas_call x1, Pallas kernels: 49.9 us -> 49.2 us  [on_device(): pl.pallas_call(functools.partial(kernel, nz, nyh, nq, np_, scale, root_k)...]
where the time goes in v6:
time: 51.4 us; the launch traced here: 51.3 us
  Pallas kernels  49.2 us (96%)
  local copies, waits for them, and re-layouts  1.43 us (3%)
  between operations  0.65 us (1%)
    pallas_call x1, Pallas kernels, on_device(): pl.pallas_call(functools.partial(kernel, nz, nyh, nq, np_, scale, root_k)...  49.2 us
    unnamed x2, local copies, waits for them, and re-layouts  1.32 us

profile of v6, /device:TPU:1, one launch (start us, length us, event | category | flops | bytes accessed | tf_op | source)
XLA Modules:
  0.0 51.3 jit_solution(5993119746660078992)
XLA Ops:
  0.6 49.2 %shard_map.95 = (f32[12,512]{1,0:T(8,128)S(1)}, f32[8,4,1,128]{3,2,1,0:T(1,128)S(1)}) custom-call(bf16[12,256,256]{2,1,0:T(8,128)(2,1)} %refs_0_.1, bf16[12,256,256]{2,1,0:T(8,128)(2,1)} %refs_1_.1, s32[12]{0:T(128)} %refs_2_.1, bf16[128,256]{1,0:T(8,128)(2,1)} %refs_3_.1, bf16[256,128]{1,0:T(8,128)(2,1)} %refs_4_.1, s32[2,256]{1,0:T(2,128)} %refs_5_.1, ...), custom_call_target="tpu_custom_call" | custom-call | tf_op jit(solution)/shard_map/pallas_call | solution.py:583
  49.9 0.1 reshape.11
  50.0 0.7 %copy.10 = f32[384,8]{0,1:T(8,128)} copy(f32[384,8]{1,0:T(8,128)S(1)} %reshape.11) | data formatting | bytes 24576
  50.7 0.6 %copy.12 = f32[12,512]{1,0:T(8,128)} copy(f32[12,512]{1,0:T(8,128)S(1)} %get-tuple-element.10) | data formatting | bytes 49152

commit v7 on v6

--- a/solution.py
+++ b/solution.py
@@ -411,7 +411,7 @@
 
     unfold(tx, tm, 0, 0)
     for i in range(4):
-        tp_ref[:, i * 128 : (i + 1) * 128] = tx[i]
+        tp_ref[:, i * 128 : (i + 1) * 128] = tx[i, 0:el, :]
     arrived(2, nz - 5 if second_hop else nz - 3).wait_recv()
 
     def narrow(i, carry):
@@ -438,7 +438,7 @@
 
     for y in range(nyh):
         unfold(lt, tg, y * el, y * np_ * each)
-    train = jnp.concatenate([lt[i] for i in range(4)], axis=1)
+    train = jnp.concatenate([lt[i, 0 : nyh * el, :] for i in range(4)], axis=1)
     rows = nyh * el
     scores = dot(jnp.concatenate(split(train), axis=0), vb[...], NT)
     scores = scores[:rows] + scores[rows:]
@@ -562,15 +562,15 @@
         pltpu.VMEM((2, el // 2, tokens, width), F32),
         pltpu.VMEM((2, el // 2, tokens, width), F32),
         pltpu.VMEM((2, el // 2, tokens, width), BF16),
-        pltpu.VMEM((nyh * 4 * el, 128), F32),
-        pltpu.VMEM((4 * el, 128), F32),
-        pltpu.VMEM((4, el, 128), F32),
-        pltpu.VMEM((4, nyh * el, 128), F32),
+        pltpu.VMEM(((nyh + 1) * 4 * el, 128), F32),
+        pltpu.VMEM((8 * el, 128), F32),
+        pltpu.VMEM((4, 2 * el, 128), F32),
+        pltpu.VMEM((4, (nyh + 2) * el, 128), F32),
         pltpu.VMEM((nz, vl, kl), F32),
         pltpu.VMEM((nz * vl, kl), BF16),
         pltpu.VMEM((1, 1, nz * vl), F32),
         pltpu.VMEM((nmp - 1, 1, nz * vl), F32),
-        pltpu.VMEM((nmp, 8, hv), F32),
+        pltpu.VMEM((nmp + 1, 8, hv), F32),
         pltpu.VMEM((nmp - 1, 8, hv), F32),
         pltpu.VMEM((nyh * nmp, 1, 128), F32),
         pltpu.VMEM((nz, nmp // 4, 1, 128), F32),

time: 51.4 us -> 51.5 us (level)
  no operation moved by 1% of the time
where the time goes in v7:
time: 51.5 us; the launch traced here: 51.3 us
  Pallas kernels  49.3 us (96%)
  local copies, waits for them, and re-layouts  1.43 us (3%)
  between operations  0.65 us (1%)
    pallas_call x1, Pallas kernels, on_device(): pl.pallas_call(functools.partial(kernel, nz, nyh, nq, np_, scale, root_k)...  49.3 us
    unnamed x2, local copies, waits for them, and re-layouts  1.32 us

profile of v7, /device:TPU:1, one launch (start us, length us, event | category | flops | bytes accessed | tf_op | source)
XLA Modules:
  0.0 51.3 jit_solution(435297339418992778)
XLA Ops:
  0.6 49.3 %shard_map.95 = (f32[12,512]{1,0:T(8,128)S(1)}, f32[8,4,1,128]{3,2,1,0:T(1,128)S(1)}) custom-call(bf16[12,256,256]{2,1,0:T(8,128)(2,1)} %refs_0_.1, bf16[12,256,256]{2,1,0:T(8,128)(2,1)} %refs_1_.1, s32[12]{0:T(128)} %refs_2_.1, bf16[128,256]{1,0:T(8,128)(2,1)} %refs_3_.1, bf16[256,128]{1,0:T(8,128)(2,1)} %refs_4_.1, s32[2,256]{1,0:T(2,128)} %refs_5_.1, ...), custom_call_target="tpu_custom_call" | custom-call | tf_op jit(solution)/shard_map/pallas_call | solution.py:583
  49.9 0.1 reshape.11
  50.0 0.7 %copy.10 = f32[384,8]{0,1:T(8,128)} copy(f32[384,8]{1,0:T(8,128)S(1)} %reshape.11) | data formatting | bytes 24576
  50.7 0.6 %copy.12 = f32[12,512]{1,0:T(8,128)} copy(f32[12,512]{1,0:T(8,128)S(1)} %get-tuple-element.10) | data formatting | bytes 49152
